TPU v7x, 32 devices: a whole 2x2x4 slice. The times are simulated.
32 devices in a mesh: groups: 2 (over y), lat: 4 (over z), chan: 2 (over x), lon: 2 (over core).
Axes of the slice: x: 2, y: 2, z: 4, core: 2. Of those that a mesh axis runs over, the one named last changes fastest.
Arguments:
- field_in: bfloat16 [1440, 24, 640], P(('groups', 'lon'), ('lat', 'chan')), parts along dimension 0, may hold values from -6 to 6
- cotangent: bfloat16 [1440, 24, 640], P(('groups', 'lon'), ('lat', 'chan')), parts along dimension 0, may hold values from -6 to 6
- mlp_in_weight: bfloat16 [640, 640], P('chan'), may hold values from -0.25 to 0.25
- mlp_out_weight: bfloat16 [640, 640], P('chan'), may hold values from -0.25 to 0.25
- legendre_analysis: bfloat16 [2, 128, 240, 24], P('lon', ('lat', 'chan')), may hold values from -1.25 to 1.25
- legendre_synthesis: bfloat16 [2, 128, 24, 240], P('lon', ('lat', 'chan')), may hold values from -0.375 to 0.375
- spectral_gain: bfloat16 [240, 640], replicated, may hold values from -1.5 to 1.5
- disco_filter: bfloat16 [120, 2, 256], P(('lat', 'chan'), None, 'lon'), may hold values from -3 to 3
- slot_pairs: int32 [120, 2], P(('lat', 'chan')), may hold values from 0 to 4, as said below
- slot_count: int32 [8], P(('lat', 'chan')), may hold values from 9 to 15
Outputs:
- field_grad: bfloat16 [1440, 24, 640], P(('groups', 'lon'), ('lat', 'chan')), parts along dimension 0
There are 2 independent parts, one for each index of `groups`. A program takes and returns all parts, laid end to end along the dimension named above; an argument that names none is the same for every part. Nothing has to cross between parts.
Inputs may be any that keep to these rules, and one draw needn't show every extreme that they name: `slot_pairs`: slots b * 15 to b * 15 + 14 belong to band b. A slot holds an output row r within the band (first entry, below 3) and an offset q of 0 to 2 * 2 (second entry): its input row lies q - 2 rows from the output row, within the band's window of 7 rows that begins 2 rows before the band. Among the first slot_count[b] slots of a band no pair repeats; the band's later slots are not used.
All inputs are finite; a program needn't handle non-finite values.
Results may differ from a plain program's by a relative error of at most 0.01.
Values may be sent and summed in bfloat16 or wider, within the bound.
A program may use at most 64 MiB of HBM per device.

v0:
```python
import math

import jax
import jax.numpy as jnp
from jax import lax
from jax.sharding import PartitionSpec as P

NLON = 720
MODES = 256
REACH = 2


def padded(cells, sides, width):
    for axis, dim in sides:
        count = lax.axis_size(axis)
        ends = count - 1
        head = lax.slice_in_dim(cells, 0, width, axis=dim)
        tail = lax.slice_in_dim(cells, cells.shape[dim] - width, cells.shape[dim], axis=dim)
        cells = jnp.concatenate(
            [
                lax.ppermute(tail, axis, [(i, (i + 1) % count) for i in range(ends)]),
                cells,
                lax.ppermute(head, axis, [((i + 1) % count, i) for i in range(ends)]),
            ],
            axis=dim,
        )
    return cells


def gelu_slope(inputs):
    normal_cdf = 0.5 * (1.0 + jax.scipy.special.erf(inputs * (1.0 / math.sqrt(2.0))))
    normal_pdf = jnp.exp(-0.5 * inputs * inputs) * (1.0 / math.sqrt(2.0 * math.pi))
    return normal_cdf + inputs * normal_pdf


def lon_tables(lon_ids, mode_ids):
    phase_index = lon_ids[:, None] * mode_ids[None, :] % NLON
    angle_rad = phase_index.astype(jnp.float32) * (2.0 * math.pi / NLON)
    return jnp.stack([jnp.cos(angle_rad), -jnp.sin(angle_rad)], axis=-1).astype(jnp.bfloat16)


def to_spectrum(grid_block):
    half_modes = MODES // lax.axis_size("lon")
    mode_ids = lax.axis_index("lon") * half_modes + jnp.arange(half_modes, dtype=jnp.int32)
    tail_shape = grid_block.shape[1:]
    piece_block = lax.all_gather(grid_block, "lon", axis=0, tiled=True)
    lon_count = piece_block.shape[0]
    lon_ids = jnp.arange(lon_count, dtype=jnp.int32)
    table_flat = lon_tables(lon_ids, mode_ids).reshape(lon_count, 2 * half_modes)
    summed = lax.dot_general(
        table_flat, piece_block, (((0,), (0,)), ((), ())), preferred_element_type=jnp.float32
    )
    return (
        (summed * (1.0 / math.sqrt(NLON)))
        .reshape((half_modes, 2) + tail_shape)
        .astype(jnp.bfloat16)
    )


def to_grid(band_block):
    lon_local = NLON // lax.axis_size("lon")
    lon_ids = lax.axis_index("lon") * lon_local + jnp.arange(lon_local, dtype=jnp.int32)
    tail_shape = band_block.shape[2:]
    piece_block = lax.all_gather(band_block, "lon", axis=0, tiled=True)
    mode_count = piece_block.shape[0]
    mode_ids = jnp.arange(mode_count, dtype=jnp.int32)
    table_flat = lon_tables(lon_ids, mode_ids).reshape(lon_local, 2 * mode_count)
    stacked = piece_block.reshape((2 * mode_count,) + tail_shape)
    summed = lax.dot_general(
        table_flat, stacked, (((1,), (0,)), ((), ())), preferred_element_type=jnp.float32
    )
    return summed * (1.0 / math.sqrt(NLON))


def to_owners(band_block):
    return lax.all_to_all(band_block, ("lat", "chan"), split_axis=0, concat_axis=2, tiled=True)


def to_bands(owned_block):
    return lax.all_to_all(owned_block, ("lat", "chan"), split_axis=2, concat_axis=0, tiled=True)


def disco_bands(spectrum, disco_filter, slot_pairs, slot_count):
    widened = padded(spectrum, ((("lat", "chan"), 2),), REACH)

    def add_slot(slot_index, running):
        out_row = slot_pairs[slot_index, 0]
        offset_col = slot_pairs[slot_index, 1]
        source = lax.dynamic_slice_in_dim(widened, out_row + offset_col, 1, 2).astype(jnp.float32)
        weights = disco_filter[slot_index].astype(jnp.float32)
        real_weight = weights[0][:, None, None]
        imag_weight = weights[1][:, None, None]
        real_part = real_weight * source[:, 0] - imag_weight * source[:, 1]
        imag_part = real_weight * source[:, 1] + imag_weight * source[:, 0]
        current = lax.dynamic_slice_in_dim(running, out_row, 1, 2)
        updated = current + jnp.stack([real_part, imag_part], axis=1)
        return lax.dynamic_update_slice_in_dim(running, updated, out_row, 2)

    initial = jnp.zeros(spectrum.shape, jnp.float32)
    return lax.fori_loop(0, slot_count[0], add_slot, initial).astype(jnp.bfloat16)


def disco_bands_adjoint(grad_block, disco_filter, slot_pairs, slot_count):
    band_rows = grad_block.shape[2]

    def add_slot(slot_index, running):
        out_row = slot_pairs[slot_index, 0]
        offset_col = slot_pairs[slot_index, 1]
        grad_row = lax.dynamic_slice_in_dim(grad_block, out_row, 1, 2).astype(jnp.float32)
        weights = disco_filter[slot_index].astype(jnp.float32)
        real_weight = weights[0][:, None, None]
        imag_weight = weights[1][:, None, None]
        real_part = real_weight * grad_row[:, 0] + imag_weight * grad_row[:, 1]
        imag_part = real_weight * grad_row[:, 1] - imag_weight * grad_row[:, 0]
        target_row = out_row + offset_col
        current = lax.dynamic_slice_in_dim(running, target_row, 1, 2)
        updated = current + jnp.stack([real_part, imag_part], axis=1)
        return lax.dynamic_update_slice_in_dim(running, updated, target_row, 2)

    widened_shape = grad_block.shape[:2] + (band_rows + 2 * REACH,) + grad_block.shape[3:]
    spread = lax.fori_loop(0, slot_count[0], add_slot, jnp.zeros(widened_shape, jnp.float32))
    rim_rows = jnp.concatenate([spread[:, :, :REACH], spread[:, :, band_rows + REACH :]], axis=2)
    folded = padded(rim_rows.astype(jnp.bfloat16), ((("lat", "chan"), 2),), REACH).astype(
        rim_rows.dtype
    )
    own_rows = spread[:, :, REACH : REACH + band_rows]
    pad_rows = band_rows - REACH
    from_above = jnp.pad(folded[:, :, :REACH], ((0, 0), (0, 0), (0, pad_rows), (0, 0)))
    from_below = jnp.pad(folded[:, :, 3 * REACH :], ((0, 0), (0, 0), (pad_rows, 0), (0, 0)))
    return (own_rows + from_above + from_below).astype(jnp.bfloat16)


def per_device(
    field_in,
    cotangent,
    mlp_in_weight,
    mlp_out_weight,
    legendre_analysis,
    legendre_synthesis,
    spectral_gain,
    disco_filter,
    slot_pairs,
    slot_count,
):
    analysis = legendre_analysis.reshape(legendre_analysis.shape[1:])
    synthesis = legendre_synthesis.reshape(legendre_synthesis.shape[1:])
    gain_table = spectral_gain.astype(jnp.float32)
    channels = field_in.shape[2]
    weight_in, weight_out = (
        lax.all_gather(mlp_in_weight, "chan", axis=0, tiled=True),
        lax.all_gather(mlp_out_weight, "chan", axis=0, tiled=True),
    )
    mixed_band = disco_bands(to_spectrum(field_in), disco_filter, slot_pairs, slot_count)
    mixed = to_owners(mixed_band)
    coeffs = jnp.einsum("kla,krac->krlc", analysis, mixed, preferred_element_type=jnp.float32)
    filtered = (coeffs * gain_table).astype(jnp.bfloat16)
    synthesized = jnp.einsum(
        "kal,krlc->krac", synthesis, filtered, preferred_element_type=jnp.float32
    ).astype(jnp.bfloat16)
    spatial = to_grid(to_bands(synthesized))
    hidden_in = (field_in.astype(jnp.float32) + spatial).astype(jnp.bfloat16)
    hidden_rows = hidden_in.reshape(-1, channels)
    pre_act = jnp.dot(hidden_rows, weight_in, preferred_element_type=jnp.float32)
    grad_rows = cotangent.reshape(-1, channels)
    grad_act = lax.dot_general(
        grad_rows, weight_out, (((1,), (1,)), ((), ())), preferred_element_type=jnp.float32
    )
    grad_pre = (grad_act * gelu_slope(pre_act)).astype(jnp.bfloat16)
    back_rows = lax.dot_general(
        grad_pre, weight_in, (((1,), (1,)), ((), ())), preferred_element_type=jnp.float32
    )
    grad_hidden = (grad_rows.astype(jnp.float32) + back_rows).astype(jnp.bfloat16)
    grad_grid = grad_hidden.reshape(cotangent.shape)
    grad_owned = to_owners(to_spectrum(grad_grid))
    grad_coeffs = jnp.einsum(
        "kal,krac->krlc", synthesis, grad_owned, preferred_element_type=jnp.float32
    )
    grad_filtered = (grad_coeffs * gain_table).astype(jnp.bfloat16)
    grad_mixed = jnp.einsum(
        "kla,krlc->krac", analysis, grad_filtered, preferred_element_type=jnp.float32
    ).astype(jnp.bfloat16)
    grad_band = disco_bands_adjoint(to_bands(grad_mixed), disco_filter, slot_pairs, slot_count)
    grad_spatial = to_grid(grad_band)
    return (grad_grid.astype(jnp.float32) + grad_spatial).astype(jnp.bfloat16)


def solution(mesh):
    return jax.shard_map(
        per_device,
        mesh=mesh,
        in_specs=(
            P(("groups", "lon"), ("lat", "chan"), None),
            P(("groups", "lon"), ("lat", "chan"), None),
            P("chan", None),
            P("chan", None),
            P("lon", ("lat", "chan"), None, None),
            P("lon", ("lat", "chan"), None, None),
            P(),
            P(("lat", "chan"), None, "lon"),
            P(("lat", "chan"), None),
            P(("lat", "chan")),
        ),
        out_specs=P(("groups", "lon"), ("lat", "chan"), None),
        check_vma=False,
    )
```

profile of v0, /device:TPU:1, one launch (start us, length us, event | category | flops | bytes accessed | tf_op | source)
XLA Modules:
  0.0 526.3 jit_solution(13503960764849112480)
XLA Ops:
  9.9 13.0 %all-gather.5.cloned.1.call-done = bf16[720,3,640]{2,0,1:T(8,128)(2,1)} async-done(((bf16[360,3,640]{2,0,1:T(8,128)(2,1)}), bf16[720,3,640]{2,0,1:T(8,128)(2,1)}) %all-gather.5.cloned.1.call-update) | async-done | bytes 2764816 | tf_op jit(solution)/shard_map/all_gather | solution.py:46
  27.2 3.5 collective-permute-start
  32.0 26.9 %collective-permute-done = bf16[128,2,2,640]{3,0,2,1:T(8,128)(2,1)S(1)} collective-permute-done((bf16[128,2,2,640]{3,0,2,1:T(8,128)(2,1)}, bf16[128,2,2,640]{3,0,2,1:T(8,128)(2,1)S(1)}, u32[]{:S(2)}, u32[]{:S(2)}) %collective-permute-start) | collective-permute-done | bytes 655392 | tf_op jit(solution)/shard_map/ppermute | solution.py:21
  61.1 111.1 %while.20 = (s32[]{:T(128)}, f32[128,2,3,640]{3,1,2,0:T(2,128)S(1)}, s32[]{:T(128)}, s32[15,2]{0,1:T(2,128)S(1)}, bf16[15,2,128]{2,1,0:T(2,128)(2,1)}, /*index=5...) while((s32[]{:T(128)}, ...), condition=%wide.region_1.2_spmd, body=%wide.region_0.1_spmd.sunk | while | flops 983308 | bytes 6886155 | solution.py:100
  173.9 5.6 %all-to-all-start = ((bf16[128,2,3,640]{3,1,2,0:T(2,128)(2,1)}), bf16[128,2,3,640]{3,1,2,0:T(2,128)(2,1)S(1)}, u32[]{:S(2)}, u32[]{:S(2)}) async-start(bf16[128,2,3,640]{3,1,2,0:T(2,128)(2,1)} %convert_element_type.127), calls=%async_computation | async-start | bytes 1966080 | tf_op jit(solution)/shard_map/all_to_all | solution.py:76
  179.6 23.6 %all-to-all-done = bf16[128,2,3,640]{3,1,2,0:T(2,128)(2,1)S(1)} async-done(((bf16[128,2,3,640]{3,1,2,0:T(2,128)(2,1)}), bf16[128,2,3,640]{3,1,2,0:T(2,128)(2,1)S(1)}, u32[]{:S(2)}, u32[]{:S(2)}) %all-to-all-start) | async-done | bytes 983072 | tf_op jit(solution)/shard_map/all_to_all | solution.py:76
  203.4 4.0 fusion.35
  208.2 27.9 %all_to_all.72 = bf16[16,2,24,640]{3,1,0,2:T(2,128)(2,1)S(1)} all-to-all(bf16[16,2,24,640]{3,1,0,2:T(2,128)(2,1)S(1)} %copy.122), channel_id=1, replica_groups=mesh['groups'=2,'lat'=4,'chan'=2,'lon'=2] {'lat','chan'}, dimensions={2} | all-to-all | bytes 1966080 | tf_op jit(solution)/shard_map/all_to_all | solution.py:80
  240.9 12.4 %all_gather.21 = bf16[640,640]{1,0:T(8,128)(2,1)} all-gather(bf16[320,640]{1,0:T(8,128)(2,1)} %param.16), channel_id=1, replica_groups=mesh['groups'=2,'lat'=4,'chan'=2,'lon'=2] {'chan'}, dimensions={0}, use_global_device_ids=true | all-gather | bytes 1228800 | tf_op jit(solution)/shard_map/all_gather | solution.py:150
  253.2 9.8 %all_gather.18 = bf16[640,640]{1,0:T(8,128)(2,1)} all-gather(bf16[320,640]{1,0:T(8,128)(2,1)} %param.17), channel_id=1, replica_groups=mesh['groups'=2,'lat'=4,'chan'=2,'lon'=2] {'chan'}, dimensions={0}, use_global_device_ids=true | all-gather | bytes 1228800 | tf_op jit(solution)/shard_map/all_gather | solution.py:151
  270.0 4.2 fusion.73
  274.3 5.5 %fusion.17 = bf16[1080,640]{1,0:T(8,128)(2,1)S(1)} fusion(bf16[640,640]{1,0:T(8,128)(2,1)} %all_gather.21, bf16[1080,640]{1,0:T(8,128)(2,1)S(1)} %copy-done.4, bf16[640,640]{1,0:T(8,128)(2,1)} %all_gather.18, f32[1080,640]{1,0:T(8,128)} %fusion.73), kind=kOutput, calls=%fused_computation.39 | convolution fusion | flops 1778457600 | bytes 7168000 | tf_op jit(solution)/shard_map/dot_general | solution.py:169
  281.8 15.2 %all-gather.9.cloned.1.call-done = bf16[720,3,640]{2,0,1:T(8,128)(2,1)} async-done(((bf16[360,3,640]{2,0,1:T(8,128)(2,1)}), bf16[720,3,640]{2,0,1:T(8,128)(2,1)}) %all-gather.9.cloned.1.call-update) | async-done | bytes 2764816 | tf_op jit(solution)/shard_map/all_gather | solution.py:46
  297.0 2.8 multiply_convert_fusion
  300.8 29.1 %all_to_all.73 = bf16[128,2,3,640]{3,1,2,0:T(2,128)(2,1)S(1)} all-to-all(bf16[128,2,3,640]{3,1,2,0:T(2,128)(2,1)S(1)} %copy.129), channel_id=1, replica_groups=mesh['groups'=2,'lat'=4,'chan'=2,'lon'=2] {'lat','chan'}, dimensions={0} | all-to-all | bytes 1966080 | tf_op jit(solution)/shard_map/all_to_all | solution.py:76
  331.0 4.0 fusion.38
  336.8 4.3 all-to-all-start.3
  341.1 23.2 %all-to-all-done.3 = bf16[16,2,24,640]{3,1,0,2:T(2,128)(2,1)S(1)} async-done(((bf16[16,2,24,640]{3,1,0,2:T(2,128)(2,1)}), bf16[16,2,24,640]{3,1,0,2:T(2,128)(2,1)S(1)}, u32[]{:S(2)}, u32[]{:S(2)}) %all-to-all-start.3) | async-done | bytes 983072 | tf_op jit(solution)/shard_map/all_to_all | solution.py:80
  367.1 111.2 %while.21 = (s32[]{:T(128)}, f32[128,2,7,640]{3,0,1,2:T(8,128)}, s32[]{:T(128)}, s32[15,2]{0,1:T(2,128)S(1)}, bf16[15,2,128]{2,1,0:T(2,128)(2,1)}, /*index=5*/bf...) while((s32[]{:T(128)}, f32[128,2,7,640]{3,0,1,2:T(8,128)}, ...), condition=%wide.region_3.4_spmd, body=%wide.region_2.3_spmd.sunk | while | flops 983308 | bytes 5575435 | solution.py:121
  483.7 10.9 %collective-permute-done.2 = bf16[128,2,2,640]{3,0,1,2:T(8,128)(2,1)S(1)} collective-permute-done((bf16[128,2,2,640]{3,0,1,2:T(8,128)(2,1)S(1)}, bf16[128,2,2,640]{3,0,1,2:T(8,128)(2,1)S(1)}, u32[]{:S(2)}, u32[]{:S(2)}) %collective-permute-start.2) | collective-permute-done | bytes 655392 | tf_op jit(solution)/shard_map/ppermute | solution.py:21
  494.5 3.9 collective-permute-done.3
  498.6 3.0 fusion.28
  501.6 14.7 %all-gather.11.cloned.1.call-done = bf16[256,2,3,640]{3,0,1,2:T(8,128)(2,1)} async-done(((bf16[128,2,3,640]{3,0,1,2:T(8,128)(2,1)}), bf16[256,2,3,640]{3,0,1,2:T(8,128)(2,1)}) %all-gather.11.cloned.1.call-update) | async-done | bytes 1966096 | tf_op jit(solution)/shard_map/all_gather | solution.py:64
  516.3 3.6 fusion.23
  (312 shorter events, 141.7 us)
Async XLA Ops:
  6.5 196.9 %copy-start = (bf16[1,16,240,24]{2,3,1,0:T(8,128)(2,1)S(1)}, bf16[1,16,240,24]{2,3,1,0:T(8,128)(2,1)}, u32[]{:S(2)}) copy-start(bf16[1,16,240,24]{2,3,1,0:T(8,128)(2,1)} %param.18) | copy-start | bytes 552964
  6.5 16.4 %all-gather.5.cloned.1.call-start = ((), (), s32[]{:S(2)}) async-start(), calls=%async_computation.4 | async-start | bytes 4147200 | tf_op jit(solution)/shard_map/all_gather | solution.py:46
  9.9 13.0 %copy-start.7 = (bf16[720,256]{0,1:T(8,128)(2,1)}, bf16[720,256]{0,1:T(8,128)(2,1)S(1)}, u32[]{:S(2)}) copy-start(bf16[720,256]{0,1:T(8,128)(2,1)S(1)} %convert_element_type.124) | copy-start | bytes 1105924
  27.2 31.7 %collective-permute-start = (bf16[128,2,2,640]{3,0,2,1:T(8,128)(2,1)}, bf16[128,2,2,640]{3,0,2,1:T(8,128)(2,1)S(1)}, u32[]{:S(2)}, u32[]{:S(2)}) collective-permute-start(bf16[128,2,2,640]{3,0,2,1:T(8,128)(2,1)} %get-tuple-element.165), channel_id=1, source_target_pairs={{0,2},{2,4},{4,6},{6,8},{8,10},{10,12},{12,14},{1,3},{3,5},{5,7},{... | collective-permute-start | bytes 1966088 | tf_op jit(solution)/shard_map/ppermute | solution.py:21
  30.7 28.2 %collective-permute-start.1 = (bf16[128,2,2,640]{3,0,2,1:T(8,128)(2,1)S(1)}, bf16[128,2,2,640]{3,0,2,1:T(8,128)(2,1)S(1)}, u32[]{:S(2)}, u32[]{:S(2)}) collective-permute-start(bf16[128,2,2,640]{3,0,2,1:T(8,128)(2,1)S(1)} %get-tuple-element.166), channel_id=1, source_target_pairs={{2,0},{4,2},{6,4},{8,6},{10,8},{12,10},{14,12},{3,1},{5,3},{7,5},{... | collective-permute-start | bytes 1966088 | tf_op jit(solution)/shard_map/ppermute | solution.py:23
  32.0 29.2 %copy-start.14 = (s32[15,2]{0,1:T(2,128)S(1)}, s32[15,2]{0,1:T(2,128)}, u32[]{:S(2)}) copy-start(s32[15,2]{0,1:T(2,128)} %param.22) | copy-start | bytes 364
  172.2 7.3 %copy-start.9 = (bf16[240,640]{1,0:T(8,128)(2,1)S(1)}, bf16[240,640]{1,0:T(8,128)(2,1)}, u32[]{:S(2)}) copy-start(bf16[240,640]{1,0:T(8,128)(2,1)} %param.20) | copy-start | bytes 921604
  173.9 29.4 %all-to-all-start = ((bf16[128,2,3,640]{3,1,2,0:T(2,128)(2,1)}), bf16[128,2,3,640]{3,1,2,0:T(2,128)(2,1)S(1)}, u32[]{:S(2)}, u32[]{:S(2)}) async-start(bf16[128,2,3,640]{3,1,2,0:T(2,128)(2,1)} %convert_element_type.127), calls=%async_computation | async-start | bytes 1966080 | tf_op jit(solution)/shard_map/all_to_all | solution.py:76
  179.5 23.9 %copy-start.16 = (bf16[1,16,24,240]{3,2,1,0:T(8,128)(2,1)S(1)}, bf16[1,16,24,240]{3,2,1,0:T(8,128)(2,1)}, u32[]{:S(2)}) copy-start(bf16[1,16,24,240]{3,2,1,0:T(8,128)(2,1)} %param.19) | copy-start | bytes 552964
  179.5 85.4 %all-gather.7.cloned.1.call-start = ((), (), s32[]{:S(2)}) async-start(), calls=%async_computation.5 | async-start | bytes 2949120 | tf_op jit(solution)/shard_map/all_gather | solution.py:64
  179.6 27.8 %copy-start.5 = (f32[240,640]{1,0:T(8,128)}, f32[240,640]{1,0:T(8,128)S(1)}, u32[]{:S(2)}) copy-start(f32[240,640]{1,0:T(8,128)S(1)} %convert_element_type.128) | copy-start | bytes 1843204
  236.1 1.7 copy-start.3
  237.3 59.6 %all-gather.9.cloned.1.call-start = ((), (), s32[]{:S(2)}) async-start(), calls=%async_computation.6 | async-start | bytes 4147200 | tf_op jit(solution)/shard_map/all_gather | solution.py:46
  238.5 27.1 %copy-start.2 = (bf16[360,3,640]{2,0,1:T(8,128)(2,1)S(1)}, bf16[360,3,640]{2,0,1:T(8,128)(2,1)}, u32[]{:S(2)}) copy-start(bf16[360,3,640]{2,0,1:T(8,128)(2,1)} %param.14) | copy-start | bytes 4147204
  270.0 4.3 copy-start.4
  280.5 16.5 %copy-start.8 = (bf16[720,256]{0,1:T(8,128)(2,1)S(1)}, bf16[720,256]{0,1:T(8,128)(2,1)}, u32[]{:S(2)}) copy-start(bf16[720,256]{0,1:T(8,128)(2,1)} %copy-done.7) | copy-start | bytes 1105924
  336.8 27.5 %all-to-all-start.3 = ((bf16[16,2,24,640]{3,1,0,2:T(2,128)(2,1)}), bf16[16,2,24,640]{3,1,0,2:T(2,128)(2,1)S(1)}, u32[]{:S(2)}, u32[]{:S(2)}) async-start(bf16[16,2,24,640]{3,1,0,2:T(2,128)(2,1)} %copy.133), calls=%async_computation.3 | async-start | bytes 1966080 | tf_op jit(solution)/shard_map/all_to_all | solution.py:80
  341.0 175.2 %all-gather.11.cloned.1.call-start = ((), (), s32[]{:S(2)}) async-start(), calls=%async_computation.7 | async-start | bytes 2949120 | tf_op jit(solution)/shard_map/all_gather | solution.py:64
  481.0 17.5 %copy-start.15 = (pred[3]{0:T(512)(128)(4,1)S(1)}, pred[3]{0:T(512)(128)(4,1)}, u32[]{:S(2)}) copy-start(pred[3]{0:T(512)(128)(4,1)} %constant.74.clone.1) | copy-start | bytes 13
  481.0 13.5 %collective-permute-start.2 = (bf16[128,2,2,640]{3,0,1,2:T(8,128)(2,1)S(1)}, bf16[128,2,2,640]{3,0,1,2:T(8,128)(2,1)S(1)}, u32[]{:S(2)}, u32[]{:S(2)}) collective-permute-start(bf16[128,2,2,640]{3,0,1,2:T(8,128)(2,1)S(1)} %get-tuple-element.163), channel_id=1, source_target_pairs={{0,2},{2,4},{4,6},{6,8},{8,10},{10,12},{12,14},{1,3},{3,5},{5,7},{... | collective-permute-start | bytes 1966088 | tf_op jit(solution)/shard_map/ppermute | solution.py:21
  482.4 16.0 %collective-permute-start.3 = (bf16[128,2,2,640]{3,0,1,2:T(8,128)(2,1)S(1)}, bf16[128,2,2,640]{3,0,1,2:T(8,128)(2,1)S(1)}, u32[]{:S(2)}, u32[]{:S(2)}) collective-permute-start(bf16[128,2,2,640]{3,0,1,2:T(8,128)(2,1)S(1)} %get-tuple-element.164), channel_id=1, source_target_pairs={{2,0},{4,2},{6,4},{8,6},{10,8},{12,10},{14,12},{3,1},{5,3},{7,5},{... | collective-permute-start | bytes 1966088 | tf_op jit(solution)/shard_map/ppermute | solution.py:23
  498.5 17.7 %copy-start.1 = (bf16[360,3,640]{2,0,1:T(8,128)(2,1)S(1)}, bf16[360,3,640]{2,0,1:T(8,128)(2,1)}, u32[]{:S(2)}) copy-start(bf16[360,3,640]{2,0,1:T(8,128)(2,1)} %copy.126) | copy-start | bytes 4147204
  498.5 17.7 %copy-start.11 = (bf16[360,256,1]{1,0,2:T(8,128)(2,1)S(1)}, bf16[360,256,1]{1,0,2:T(8,128)(2,1)}, u32[]{:S(2)}) copy-start(bf16[360,256,1]{1,0,2:T(8,128)(2,1)} %copy-done.10) | copy-start | bytes 552964
  498.5 17.7 %copy-start.13 = (bf16[360,256,1]{1,0,2:T(8,128)(2,1)S(1)}, bf16[360,256,1]{1,0,2:T(8,128)(2,1)}, u32[]{:S(2)}) copy-start(bf16[360,256,1]{1,0,2:T(8,128)(2,1)} %copy-done.12) | copy-start | bytes 552964
  (4 other events, 3.6 us)
Sparse Core Ops, SparseCore 0:
  8.9 14.0 all-gather.4
  237.4 10.7 all-gather.6
  281.9 15.0 all-gather.8
  501.7 14.4 all-gather.10
where the time goes:
time: 537 us; the launch traced here: 526 us
  waiting for transfers between devices  132 us (25%)
  loops' own time  120 us (22%)
  blocking collectives  79.1 us (15%)
  other arithmetic  67.7 us (13%)
  local copies, waits for them, and re-layouts  66.8 us (12%)
  matrix products  29.3 us (5%)
  starting transfers between devices  17.6 us (3%)
  between operations  13.6 us (3%)
    another operation x1, loops' own time, disco_bands(): lax.fori_loop(0, slot_count[0], add_slot, initial).astype(jnp.bfloat16)  62.4 us
    another operation x1, loops' own time, disco_bands_adjoint(): lax.fori_loop(0, slot_count[0], add_slot, jnp.zeros(widened_shape, jnp.fl...  57.7 us
    ppermute x2, waiting for transfers between devices, padded(): lax.ppermute(tail, axis, [(i, (i + 1) % count) for i in range(ends)])  37.8 us
    all_to_all x1, blocking collectives, to_owners(): lax.all_to_all(band_block, ('lat', 'chan'), split_axis=0, concat_axis=2,...  29.1 us
    all_gather x2, waiting for transfers between devices, to_spectrum(): piece_block = lax.all_gather(grid_block, 'lon', axis=0, tiled=True)  28.2 us
    all_to_all x1, blocking collectives, to_bands(): lax.all_to_all(owned_block, ('lat', 'chan'), split_axis=2, concat_axis=0,...  27.9 us
    all_to_all x1, waiting for transfers between devices, to_owners(): lax.all_to_all(band_block, ('lat', 'chan'), split_axis=0, concat_axis=2,...  23.6 us
    all_to_all x1, waiting for transfers between devices, to_bands(): lax.all_to_all(owned_block, ('lat', 'chan'), split_axis=2, concat_axis=0,...  23.2 us
  transfers between devices with their start and end apart: 10, of which 8 were waited for; matrix products, arithmetic and copies ran while one was open for 1% of the time, Pallas kernels for 0%

commit v1 on v0

--- a/solution.py
+++ b/solution.py
@@ -8,23 +8,6 @@
 NLON = 720
 MODES = 256
 REACH = 2
-
-
-def padded(cells, sides, width):
-    for axis, dim in sides:
-        count = lax.axis_size(axis)
-        ends = count - 1
-        head = lax.slice_in_dim(cells, 0, width, axis=dim)
-        tail = lax.slice_in_dim(cells, cells.shape[dim] - width, cells.shape[dim], axis=dim)
-        cells = jnp.concatenate(
-            [
-                lax.ppermute(tail, axis, [(i, (i + 1) % count) for i in range(ends)]),
-                cells,
-                lax.ppermute(head, axis, [((i + 1) % count, i) for i in range(ends)]),
-            ],
-            axis=dim,
-        )
-    return cells
 
 
 def gelu_slope(inputs):
@@ -80,54 +63,28 @@
     return lax.all_to_all(owned_block, ("lat", "chan"), split_axis=2, concat_axis=0, tiled=True)
 
 
-def disco_bands(spectrum, disco_filter, slot_pairs, slot_count):
-    widened = padded(spectrum, ((("lat", "chan"), 2),), REACH)
-
-    def add_slot(slot_index, running):
-        out_row = slot_pairs[slot_index, 0]
-        offset_col = slot_pairs[slot_index, 1]
-        source = lax.dynamic_slice_in_dim(widened, out_row + offset_col, 1, 2).astype(jnp.float32)
-        weights = disco_filter[slot_index].astype(jnp.float32)
-        real_weight = weights[0][:, None, None]
-        imag_weight = weights[1][:, None, None]
-        real_part = real_weight * source[:, 0] - imag_weight * source[:, 1]
-        imag_part = real_weight * source[:, 1] + imag_weight * source[:, 0]
-        current = lax.dynamic_slice_in_dim(running, out_row, 1, 2)
-        updated = current + jnp.stack([real_part, imag_part], axis=1)
-        return lax.dynamic_update_slice_in_dim(running, updated, out_row, 2)
-
-    initial = jnp.zeros(spectrum.shape, jnp.float32)
-    return lax.fori_loop(0, slot_count[0], add_slot, initial).astype(jnp.bfloat16)
+def band_filter(disco_filter, slot_pairs, slot_count, band_rows):
+    width = 2 * REACH + 1
+    in_use = jnp.arange(disco_filter.shape[0], dtype=jnp.int32) < slot_count[0]
+    cell_of = slot_pairs[:, 0] * width + slot_pairs[:, 1]
+    cells = jnp.arange(band_rows * width, dtype=jnp.int32)
+    chosen = ((cells[:, None] == cell_of[None, :]) & in_use[None, :]).astype(jnp.bfloat16)
+    return jnp.einsum(
+        "ts,spk->tpk", chosen, disco_filter, preferred_element_type=jnp.float32
+    ).astype(jnp.bfloat16)
 
 
-def disco_bands_adjoint(grad_block, disco_filter, slot_pairs, slot_count):
-    band_rows = grad_block.shape[2]
-
-    def add_slot(slot_index, running):
-        out_row = slot_pairs[slot_index, 0]
-        offset_col = slot_pairs[slot_index, 1]
-        grad_row = lax.dynamic_slice_in_dim(grad_block, out_row, 1, 2).astype(jnp.float32)
-        weights = disco_filter[slot_index].astype(jnp.float32)
-        real_weight = weights[0][:, None, None]
-        imag_weight = weights[1][:, None, None]
-        real_part = real_weight * grad_row[:, 0] + imag_weight * grad_row[:, 1]
-        imag_part = real_weight * grad_row[:, 1] - imag_weight * grad_row[:, 0]
-        target_row = out_row + offset_col
-        current = lax.dynamic_slice_in_dim(running, target_row, 1, 2)
-        updated = current + jnp.stack([real_part, imag_part], axis=1)
-        return lax.dynamic_update_slice_in_dim(running, updated, target_row, 2)
-
-    widened_shape = grad_block.shape[:2] + (band_rows + 2 * REACH,) + grad_block.shape[3:]
-    spread = lax.fori_loop(0, slot_count[0], add_slot, jnp.zeros(widened_shape, jnp.float32))
-    rim_rows = jnp.concatenate([spread[:, :, :REACH], spread[:, :, band_rows + REACH :]], axis=2)
-    folded = padded(rim_rows.astype(jnp.bfloat16), ((("lat", "chan"), 2),), REACH).astype(
-        rim_rows.dtype
+def filter_matrices(cells, rows):
+    width = 2 * REACH + 1
+    by_row = cells.reshape(rows, width, 2, cells.shape[2])
+    total = 0.0
+    for offset in range(width):
+        shifted = jnp.eye(rows, k=offset - REACH, dtype=jnp.bfloat16)
+        total = total + jnp.transpose(by_row[:, offset], (2, 1, 0))[:, :, :, None] * shifted
+    real, imag = total[:, 0], total[:, 1]
+    return jnp.concatenate(
+        [jnp.concatenate([real, -imag], axis=2), jnp.concatenate([imag, real], axis=2)], axis=1
     )
-    own_rows = spread[:, :, REACH : REACH + band_rows]
-    pad_rows = band_rows - REACH
-    from_above = jnp.pad(folded[:, :, :REACH], ((0, 0), (0, 0), (0, pad_rows), (0, 0)))
-    from_below = jnp.pad(folded[:, :, 3 * REACH :], ((0, 0), (0, 0), (pad_rows, 0), (0, 0)))
-    return (own_rows + from_above + from_below).astype(jnp.bfloat16)
 
 
 def per_device(
@@ -150,8 +107,25 @@
         lax.all_gather(mlp_in_weight, "chan", axis=0, tiled=True),
         lax.all_gather(mlp_out_weight, "chan", axis=0, tiled=True),
     )
-    mixed_band = disco_bands(to_spectrum(field_in), disco_filter, slot_pairs, slot_count)
-    mixed = to_owners(mixed_band)
+    cells = band_filter(disco_filter, slot_pairs, slot_count, field_in.shape[1])
+    modes_owned = analysis.shape[0]
+    rows = analysis.shape[2]
+    all_cells = lax.all_gather(cells, ("lat", "chan"), axis=0, tiled=True)
+    own_cells = lax.dynamic_slice_in_dim(
+        all_cells, lax.axis_index(("lat", "chan")) * modes_owned, modes_owned, 2
+    )
+    filters = filter_matrices(own_cells, rows)
+    owned = to_owners(to_spectrum(field_in))
+    mixed = (
+        jnp.einsum(
+            "kxy,kyc->kxc",
+            filters,
+            owned.reshape(modes_owned, 2 * rows, channels),
+            preferred_element_type=jnp.float32,
+        )
+        .astype(jnp.bfloat16)
+        .reshape(owned.shape)
+    )
     coeffs = jnp.einsum("kla,krac->krlc", analysis, mixed, preferred_element_type=jnp.float32)
     filtered = (coeffs * gain_table).astype(jnp.bfloat16)
     synthesized = jnp.einsum(
@@ -179,8 +153,17 @@
     grad_mixed = jnp.einsum(
         "kla,krlc->krac", analysis, grad_filtered, preferred_element_type=jnp.float32
     ).astype(jnp.bfloat16)
-    grad_band = disco_bands_adjoint(to_bands(grad_mixed), disco_filter, slot_pairs, slot_count)
-    grad_spatial = to_grid(grad_band)
+    grad_source = (
+        jnp.einsum(
+            "kxy,kxc->kyc",
+            filters,
+            grad_mixed.reshape(modes_owned, 2 * rows, channels),
+            preferred_element_type=jnp.float32,
+        )
+        .astype(jnp.bfloat16)
+        .reshape(grad_mixed.shape)
+    )
+    grad_spatial = to_grid(to_bands(grad_source))
     return (grad_grid.astype(jnp.float32) + grad_spatial).astype(jnp.bfloat16)
 
 

time: 537 us -> 250 us (0.47); the launches traced: 526 us -> 249 us
  loops' own time: 120 us -> 0 us
  waiting for transfers between devices: 132 us -> 48.7 us
  other arithmetic: 67.7 us -> 5.22 us
  local copies, waits for them, and re-layouts: 66.8 us -> 16.3 us
  blocking collectives: 79.1 us -> 128 us
  starting transfers between devices: 17.6 us -> 5.2 us
    another operation x2 -> x0, loops' own time: 120 us -> none  [the longest x1 62.4 us: disco_bands(): lax.fori_loop(0, slot_count[0], add_slot, initial).astype(jnp.bfloat16)]
    ppermute x4 -> x0, waiting for transfers between devices: 41.7 us -> none  [the longest x2 37.8 us: padded(): lax.ppermute(tail, axis, [(i, (i + 1) % count) for i in range(ends)])]
    convert_element_type x63 -> x3, other arithmetic: 40.7 us -> 0.22 us  [filter_matrices(): shifted = jnp.eye(rows, k=offset - REACH, dtype=jnp.bfloat16)]
    dynamic_slice x60 -> x1, local copies, waits for them, and re-layouts: 38.1 us -> 0.13 us  [per_device(): lax.dynamic_slice_in_dim(all_cells, lax.axis_index(('lat', 'chan')) * mod...]
    all_to_all x1 -> x2, blocking collectives: 27.9 us -> 53.5 us  [to_bands(): lax.all_to_all(owned_block, ('lat', 'chan'), split_axis=2, concat_axis=0,...]
    all_gather x0 -> x1, blocking collectives: none -> 25.6 us  [per_device(): all_cells = lax.all_gather(cells, ('lat', 'chan'), axis=0, tiled=True)]
    all_to_all x1 -> x0, waiting for transfers between devices: 23.2 us -> none  [to_bands(): lax.all_to_all(owned_block, ('lat', 'chan'), split_axis=2, concat_axis=0,...]
    dynamic_update_slice x15 -> x0, other arithmetic: 13.8 us -> none  [add_slot(): return lax.dynamic_update_slice_in_dim(running, updated, target_row, 2)]
  transfers between devices with their start and end apart: 10 -> 5, of which waited for: 8 -> 3; matrix products, arithmetic and copies ran while one was open for 1% -> 4% of each run, Pallas kernels for 0% -> 0%
where the time goes in v1:
time: 250 us; the launch traced here: 249 us
  blocking collectives  128 us (51%)
  waiting for transfers between devices  48.7 us (19%)
  matrix products  31.5 us (13%)
  local copies, waits for them, and re-layouts  16.3 us (7%)
  between operations  14.3 us (6%)
  other arithmetic  5.22 us (2%)
  starting transfers between devices  5.2 us (2%)
    all_to_all x2, blocking collectives, to_bands(): lax.all_to_all(owned_block, ('lat', 'chan'), split_axis=2, concat_axis=0,...  53.5 us
    all_to_all x1, blocking collectives, to_owners(): lax.all_to_all(band_block, ('lat', 'chan'), split_axis=0, concat_axis=2,...  29.2 us
    all_gather x1, blocking collectives, per_device(): all_cells = lax.all_gather(cells, ('lat', 'chan'), axis=0, tiled=True)  25.6 us
    all_to_all x1, waiting for transfers between devices, to_owners(): lax.all_to_all(band_block, ('lat', 'chan'), split_axis=0, concat_axis=2,...  19.7 us
    all_gather x2, waiting for transfers between devices, to_spectrum(): piece_block = lax.all_gather(grid_block, 'lon', axis=0, tiled=True)  16.9 us
    all_gather x2, waiting for transfers between devices, to_grid(): piece_block = lax.all_gather(band_block, 'lon', axis=0, tiled=True)  11.3 us
    all_gather x1, blocking collectives, per_device(): lax.all_gather(mlp_in_weight, 'chan', axis=0, tiled=True)  10.8 us
    all_gather x1, blocking collectives, per_device(): lax.all_gather(mlp_out_weight, 'chan', axis=0, tiled=True)  8.82 us
  transfers between devices with their start and end apart: 5, of which 3 were waited for; matrix products, arithmetic and copies ran while one was open for 4% of the time, Pallas kernels for 0%

profile of v1, /device:TPU:1, one launch (start us, length us, event | category | flops | bytes accessed | tf_op | source)
XLA Modules:
  0.0 249.2 jit_solution(4008088815173856411)
XLA Ops:
  9.5 1.7 cosine_convert_fusion
  12.2 25.6 %all_gather.22 = bf16[120,2,128]{2,1,0:T(2,128)(2,1)S(1)} all-gather(bf16[15,2,128]{2,1,0:T(2,128)(2,1)S(1)} %copy.118), channel_id=1, replica_groups=mesh['groups'=2,'lat'=4,'chan'=2,'lon'=2] {'lat','chan'}, dimensions={0}, use_global_device_ids=true | all-gather | bytes 69120 | tf_op jit(solution)/shard_map/all_gather | solution.py:113
  38.0 2.8 %multiply_convert_fusion.1 = bf16[256,3,640]{2,0,1:T(8,128)(2,1)S(1)} fusion(bf16[720,3,640]{2,0,1:T(8,128)(2,1)} %all-gather.5.cloned.1.call-done, bf16[720,256]{0,1:T(8,128)(2,1)S(1)} %convert_element_type.147), kind=kOutput, calls=%fused_computation.26 | convolution fusion | flops 708771840 | bytes 4116480 | tf_op jit(solution)/shard_map/dot_general | solution.py:33
  41.2 1.6 copy.126
  42.8 5.1 %all-to-all-start = ((bf16[128,2,3,640]{3,1,2,0:T(2,128)(2,1)}), bf16[128,2,3,640]{3,1,2,0:T(2,128)(2,1)S(1)}, u32[]{:S(2)}, u32[]{:S(2)}) async-start(bf16[128,2,3,640]{3,1,2,0:T(2,128)(2,1)} %copy.126), calls=%async_computation | async-start | bytes 1966080 | tf_op jit(solution)/shard_map/all_to_all | solution.py:59
  49.4 19.7 %all-to-all-done = bf16[128,2,3,640]{3,1,2,0:T(2,128)(2,1)S(1)} async-done(((bf16[128,2,3,640]{3,1,2,0:T(2,128)(2,1)}), bf16[128,2,3,640]{3,1,2,0:T(2,128)(2,1)S(1)}, u32[]{:S(2)}, u32[]{:S(2)}) %all-to-all-start) | async-done | bytes 983072 | tf_op jit(solution)/shard_map/all_to_all | solution.py:59
  69.9 4.0 %fusion.28 = bf16[16,2,24,640]{3,2,1,0:T(8,128)(2,1)S(1)} fusion(f32[240,640]{1,0:T(8,128)S(1)} %convert_element_type.151, bf16[16,2,24,640]{3,2,1,0:T(8,128)(2,1)S(1)} %bitcast.142, bf16[1,16,240,24]{2,3,1,0:T(8,128)(2,1)S(1)} %copy-done, bf16[1,16,24,240]{3,2,1,0:T(8,128)(2,1)S(1)} %copy-done.18), kind=kOutput, calls=%fused_computation.31 | convolution fusion | flops 482181120 | bytes 2949120 | tf_op jit(solution)/shard_map/kal,krlc->krac/dot_general | solution.py:131
  74.7 26.1 %all_to_all.69 = bf16[16,2,24,640]{3,1,0,2:T(2,128)(2,1)S(1)} all-to-all(bf16[16,2,24,640]{3,1,0,2:T(2,128)(2,1)S(1)} %copy.130), channel_id=1, replica_groups=mesh['groups'=2,'lat'=4,'chan'=2,'lon'=2] {'lat','chan'}, dimensions={2} | all-to-all | bytes 1966080 | tf_op jit(solution)/shard_map/all_to_all | solution.py:63
  103.2 2.3 reshape.312
  105.5 10.8 %all_gather.25 = bf16[640,640]{1,0:T(8,128)(2,1)} all-gather(bf16[320,640]{1,0:T(8,128)(2,1)} %param.12), channel_id=1, replica_groups=mesh['groups'=2,'lat'=4,'chan'=2,'lon'=2] {'chan'}, dimensions={0}, use_global_device_ids=true | all-gather | bytes 1228800 | tf_op jit(solution)/shard_map/all_gather | solution.py:107
  116.3 8.8 %all_gather.21 = bf16[640,640]{1,0:T(8,128)(2,1)} all-gather(bf16[320,640]{1,0:T(8,128)(2,1)} %param.13), channel_id=1, replica_groups=mesh['groups'=2,'lat'=4,'chan'=2,'lon'=2] {'chan'}, dimensions={0}, use_global_device_ids=true | all-gather | bytes 1228800 | tf_op jit(solution)/shard_map/all_gather | solution.py:108
  125.2 1.9 cosine_convert_fusion.1
  127.8 2.5 fusion.21
  131.0 1.2 reshape.318
  132.2 4.3 %fusion.71 = f32[1080,640]{1,0:T(8,128)} fusion(bf16[1080,640]{1,0:T(8,128)(2,1)S(1)} %reshape.318, bf16[640,640]{1,0:T(8,128)(2,1)} %all_gather.25), kind=kOutput, calls=%fused_computation.103 | convolution fusion | flops 884736000 | bytes 4966400 | tf_op jit(solution)/shard_map/dot_general | solution.py:137
  136.5 5.5 %fusion.13 = bf16[1080,640]{1,0:T(8,128)(2,1)S(1)} fusion(bf16[640,640]{1,0:T(8,128)(2,1)} %all_gather.25, bf16[1080,640]{1,0:T(8,128)(2,1)S(1)} %copy-done.4, bf16[640,640]{1,0:T(8,128)(2,1)} %all_gather.21, f32[1080,640]{1,0:T(8,128)} %fusion.71), kind=kOutput, calls=%fused_computation.14 | convolution fusion | flops 1778457600 | bytes 7168000 | tf_op jit(solution)/shard_map/dot_general | solution.py:143
  142.7 1.3 copy.134
  144.0 16.9 %all-gather.9.cloned.1.call-done = bf16[720,3,640]{2,0,1:T(8,128)(2,1)} async-done(((bf16[360,3,640]{2,0,1:T(8,128)(2,1)}), bf16[720,3,640]{2,0,1:T(8,128)(2,1)}) %all-gather.9.cloned.1.call-update) | async-done | bytes 2764816 | tf_op jit(solution)/shard_map/all_gather | solution.py:29
  160.9 2.8 %multiply_convert_fusion = bf16[256,3,640]{2,0,1:T(8,128)(2,1)S(1)} fusion(bf16[720,3,640]{2,0,1:T(8,128)(2,1)} %all-gather.9.cloned.1.call-done, bf16[720,256]{0,1:T(8,128)(2,1)S(1)} %copy-done.12), kind=kOutput, calls=%fused_computation.25 | convolution fusion | flops 708771840 | bytes 4116480 | tf_op jit(solution)/shard_map/dot_general | solution.py:33
  164.8 29.2 %all_to_all.70 = bf16[128,2,3,640]{3,1,2,0:T(2,128)(2,1)S(1)} all-to-all(bf16[128,2,3,640]{3,1,2,0:T(2,128)(2,1)S(1)} %copy.137), channel_id=1, replica_groups=mesh['groups'=2,'lat'=4,'chan'=2,'lon'=2] {'lat','chan'}, dimensions={0} | all-to-all | bytes 1966080 | tf_op jit(solution)/shard_map/all_to_all | solution.py:59
  194.2 4.0 %fusion.22 = bf16[16,2,640,24]{2,3,1,0:T(8,128)(2,1)S(1)} fusion(f32[240,640]{1,0:T(8,128)S(1)} %copy-done.10, bf16[16,2,24,640]{3,0,2,1:T(8,128)(2,1)S(1)} %bitcast.141, bf16[1,16,240,24]{2,3,1,0:T(8,128)(2,1)S(1)} %copy-done, bf16[1,16,24,240]{3,2,1,0:T(8,128)(2,1)S(1)} %copy-done.19), kind=kOutput, calls=%fused_computation.27 | convolution fusion | flops 482181120 | bytes 2949120 | tf_op jit(solution)/shard_map/kla,krlc->krac/dot_general | solution.py:153
  199.3 27.4 %all_to_all.71 = bf16[16,2,24,640]{3,0,1,2:T(8,128)(2,1)S(1)} all-to-all(bf16[16,2,24,640]{3,0,1,2:T(8,128)(2,1)S(1)} %copy.142), channel_id=1, replica_groups=mesh['groups'=2,'lat'=4,'chan'=2,'lon'=2] {'lat','chan'}, dimensions={2} | all-to-all | bytes 1966080 | tf_op jit(solution)/shard_map/all_to_all | solution.py:63
  227.8 11.3 %all-gather.11.cloned.1.call-done = bf16[256,2,3,640]{3,0,1,2:T(8,128)(2,1)} async-done(((bf16[128,2,3,640]{3,0,1,2:T(8,128)(2,1)}), bf16[256,2,3,640]{3,0,1,2:T(8,128)(2,1)}) %all-gather.11.cloned.1.call-update) | async-done | bytes 1966096 | tf_op jit(solution)/shard_map/all_gather | solution.py:47
  239.1 3.6 %fusion.19 = bf16[360,3,640]{2,0,1:T(8,128)(2,1)} fusion(bf16[360,3,640]{2,0,1:T(8,128)(2,1)S(1)} %copy-done.1, bf16[256,2,3,640]{3,0,1,2:T(8,128)(2,1)} %all-gather.11.cloned.1.call-done, bf16[360,256,1]{1,0,2:T(8,128)(2,1)S(1)} %copy-done.17, bf16[360,256,1]{1,0,2:T(8,128)(2,1)S(1)} %copy-done.15), kind=kOutput, calls=%fused_computation.21 | convolution fusion | flops 711290880 | bytes 5099520 | tf_op jit(solution)/shard_map/dot_general | solution.py:52
  (94 shorter events, 14.6 us)
Async XLA Ops:
  6.5 63.3 %copy-start = (bf16[1,16,240,24]{2,3,1,0:T(8,128)(2,1)S(1)}, bf16[1,16,240,24]{2,3,1,0:T(8,128)(2,1)}, u32[]{:S(2)}) copy-start(bf16[1,16,240,24]{2,3,1,0:T(8,128)(2,1)} %param.14) | copy-start | bytes 552964
  6.5 31.5 %all-gather.5.cloned.1.call-start = ((), (), s32[]{:S(2)}) async-start(), calls=%async_computation.4 | async-start | bytes 4147200 | tf_op jit(solution)/shard_map/all_gather | solution.py:29
  12.2 25.8 %copy-start.11 = (bf16[720,256]{0,1:T(8,128)(2,1)}, bf16[720,256]{0,1:T(8,128)(2,1)S(1)}, u32[]{:S(2)}) copy-start(bf16[720,256]{0,1:T(8,128)(2,1)S(1)} %convert_element_type.147) | copy-start | bytes 1105924
  40.8 7.6 %copy-start.13 = (bf16[240,640]{1,0:T(8,128)(2,1)S(1)}, bf16[240,640]{1,0:T(8,128)(2,1)}, u32[]{:S(2)}) copy-start(bf16[240,640]{1,0:T(8,128)(2,1)} %param.16) | copy-start | bytes 921604
  42.8 26.3 %all-to-all-start = ((bf16[128,2,3,640]{3,1,2,0:T(2,128)(2,1)}), bf16[128,2,3,640]{3,1,2,0:T(2,128)(2,1)S(1)}, u32[]{:S(2)}, u32[]{:S(2)}) async-start(bf16[128,2,3,640]{3,1,2,0:T(2,128)(2,1)} %copy.126), calls=%async_computation | async-start | bytes 1966080 | tf_op jit(solution)/shard_map/all_to_all | solution.py:59
  47.9 79.2 %all-gather.7.cloned.1.call-start = ((), (), s32[]{:S(2)}) async-start(), calls=%async_computation.5 | async-start | bytes 2949120 | tf_op jit(solution)/shard_map/all_gather | solution.py:47
  48.4 21.4 %copy-start.9 = (f32[240,640]{1,0:T(8,128)}, f32[240,640]{1,0:T(8,128)S(1)}, u32[]{:S(2)}) copy-start(f32[240,640]{1,0:T(8,128)S(1)} %convert_element_type.151) | copy-start | bytes 1843204
  49.3 20.5 %copy-start.5 = (bf16[16,24,24]{2,1,0:T(8,128)(2,1)}, bf16[16,24,24]{2,1,0:T(8,128)(2,1)S(1)}, u32[]{:S(2)}) copy-start(bf16[16,24,24]{2,1,0:T(8,128)(2,1)S(1)} %get-tuple-element.5) | copy-start | bytes 55300
  49.3 20.5 %copy-start.7 = (bf16[16,24,24]{2,1,0:T(8,128)(2,1)}, bf16[16,24,24]{2,1,0:T(8,128)(2,1)S(1)}, u32[]{:S(2)}) copy-start(bf16[16,24,24]{2,1,0:T(8,128)(2,1)S(1)} %get-tuple-element.6) | copy-start | bytes 55300
  49.4 20.5 %copy-start.18 = (bf16[1,16,24,240]{3,2,1,0:T(8,128)(2,1)S(1)}, bf16[1,16,24,240]{3,2,1,0:T(8,128)(2,1)}, u32[]{:S(2)}) copy-start(bf16[1,16,24,240]{3,2,1,0:T(8,128)(2,1)} %param.15) | copy-start | bytes 552964
  100.8 1.7 copy-start.3
  102.0 58.9 %all-gather.9.cloned.1.call-start = ((), (), s32[]{:S(2)}) async-start(), calls=%async_computation.6 | async-start | bytes 4147200 | tf_op jit(solution)/shard_map/all_gather | solution.py:29
  103.2 24.6 %copy-start.2 = (bf16[360,3,640]{2,0,1:T(8,128)(2,1)S(1)}, bf16[360,3,640]{2,0,1:T(8,128)(2,1)}, u32[]{:S(2)}) copy-start(bf16[360,3,640]{2,0,1:T(8,128)(2,1)} %param.10) | copy-start | bytes 4147204
  127.0 0.7 copy-start.16
  132.2 4.3 %copy-start.4 = (bf16[1080,640]{1,0:T(8,128)(2,1)S(1)}, bf16[1080,640]{1,0:T(8,128)(2,1)}, u32[]{:S(2)}) copy-start(bf16[1080,640]{1,0:T(8,128)(2,1)} %reshape.312) | copy-start | bytes 4147204
  142.7 18.2 %copy-start.12 = (bf16[720,256]{0,1:T(8,128)(2,1)S(1)}, bf16[720,256]{0,1:T(8,128)(2,1)}, u32[]{:S(2)}) copy-start(bf16[720,256]{0,1:T(8,128)(2,1)} %copy-done.11) | copy-start | bytes 1105924
  144.0 95.2 %all-gather.11.cloned.1.call-start = ((), (), s32[]{:S(2)}) async-start(), calls=%async_computation.7 | async-start | bytes 2949120 | tf_op jit(solution)/shard_map/all_gather | solution.py:47
  164.8 29.5 %copy-start.10 = (f32[240,640]{1,0:T(8,128)S(1)}, f32[240,640]{1,0:T(8,128)}, u32[]{:S(2)}) copy-start(f32[240,640]{1,0:T(8,128)} %copy-done.9) | copy-start | bytes 1843204
  164.8 29.5 %copy-start.19 = (bf16[1,16,24,240]{3,2,1,0:T(8,128)(2,1)S(1)}, bf16[1,16,24,240]{3,2,1,0:T(8,128)(2,1)}, u32[]{:S(2)}) copy-start(bf16[1,16,24,240]{3,2,1,0:T(8,128)(2,1)} %param.15) | copy-start | bytes 552964
  194.2 4.0 %copy-start.6 = (bf16[16,24,24]{2,1,0:T(8,128)(2,1)S(1)}, bf16[16,24,24]{2,1,0:T(8,128)(2,1)}, u32[]{:S(2)}) copy-start(bf16[16,24,24]{2,1,0:T(8,128)(2,1)} %copy-done.5) | copy-start | bytes 55300
  194.2 4.0 %copy-start.8 = (bf16[16,24,24]{2,1,0:T(8,128)(2,1)S(1)}, bf16[16,24,24]{2,1,0:T(8,128)(2,1)}, u32[]{:S(2)}) copy-start(bf16[16,24,24]{2,1,0:T(8,128)(2,1)} %copy-done.7) | copy-start | bytes 55300
  199.2 39.9 %copy-start.1 = (bf16[360,3,640]{2,0,1:T(8,128)(2,1)S(1)}, bf16[360,3,640]{2,0,1:T(8,128)(2,1)}, u32[]{:S(2)}) copy-start(bf16[360,3,640]{2,0,1:T(8,128)(2,1)} %copy.134) | copy-start | bytes 4147204
  199.3 39.9 %copy-start.15 = (bf16[360,256,1]{1,0,2:T(8,128)(2,1)S(1)}, bf16[360,256,1]{1,0,2:T(8,128)(2,1)}, u32[]{:S(2)}) copy-start(bf16[360,256,1]{1,0,2:T(8,128)(2,1)} %copy-done.14) | copy-start | bytes 552964
  199.3 39.9 %copy-start.17 = (bf16[360,256,1]{1,0,2:T(8,128)(2,1)S(1)}, bf16[360,256,1]{1,0,2:T(8,128)(2,1)}, u32[]{:S(2)}) copy-start(bf16[360,256,1]{1,0,2:T(8,128)(2,1)} %copy-done.16) | copy-start | bytes 552964
  (1 other events, 0.7 us)
Sparse Core Ops, SparseCore 0:
  8.9 14.0 all-gather.4
  102.1 12.1 all-gather.6
  144.1 16.7 all-gather.8
  227.9 11.1 all-gather.10

commit v2 on v1

--- a/solution.py
+++ b/solution.py
@@ -1,8 +1,12 @@
+import functools
 import math
 
 import jax
 import jax.numpy as jnp
+import numpy as np
 from jax import lax
+from jax.experimental import pallas as pl
+from jax.experimental.pallas import tpu as pltpu
 from jax.sharding import PartitionSpec as P
 
 NLON = 720
@@ -87,7 +91,7 @@
     )
 
 
-def per_device(
+def per_device_plain(
     field_in,
     cotangent,
     mlp_in_weight,
@@ -167,9 +171,398 @@
     return (grad_grid.astype(jnp.float32) + grad_spatial).astype(jnp.bfloat16)
 
 
+def fixed_tables(bands, modes, lon_pad):
+    halves = MODES // (bands * modes)
+    lon_ids = np.arange(NLON, dtype=np.int32)
+    mode_ids = np.arange(MODES, dtype=np.int32)
+    phase_index = lon_ids[:, None] * mode_ids[None, :] % NLON
+    angle_rad = phase_index.astype(np.float32) * np.float32(2.0 * math.pi / NLON)
+    paired = np.stack([np.cos(angle_rad), -np.sin(angle_rad)], axis=0)
+    blocks = paired.reshape(2, halves, NLON // halves, halves, bands, modes)
+    blocks = blocks.transpose(3, 1, 4, 0, 5, 2).reshape(halves, halves, bands * 2 * modes, -1)
+    blocks = np.pad(blocks, ((0, 0), (0, 0), (0, 0), (0, lon_pad - blocks.shape[3])))
+    return blocks.astype(jnp.bfloat16)
+
+
+def block_kernel(
+    sizes,
+    field,
+    cot,
+    win_own,
+    wout_own,
+    pieces,
+    left,
+    right,
+    left_t,
+    right_t,
+    gain,
+    table_in,
+    table_out,
+    out,
+    other,
+    sent,
+    landed,
+    back_sent,
+    back_landed,
+    back_other,
+    pieces_all,
+    pieces_f32,
+    strided_in,
+    strided_out,
+    win,
+    wout,
+    grad_act,
+    hidden,
+    lon_sem,
+    go_sem,
+    back_sem,
+    swap_sem,
+    piece_sem,
+    weight_sem,
+):
+    bands, chans, rows, modes, channels, chunks = sizes
+    width = 2 * rows * modes
+    per_row = 2 * modes
+    total = bands * width
+    lat, chan, lon = lax.axis_index("lat"), lax.axis_index("chan"), lax.axis_index("lon")
+    me = lat * chans + chan
+    mate = {"lon": 1 - lon}
+    scale = 1.0 / math.sqrt(NLON)
+    started = []
+
+    def band_at(step):
+        band = lax.rem(me + step, bands)
+        return band, {"lat": band // chans, "chan": lax.rem(band, chans)}
+
+    def send(src, dst, sems, where):
+        copy = pltpu.make_async_remote_copy(
+            src_ref=src,
+            dst_ref=dst,
+            send_sem=sems.at[0],
+            recv_sem=sems.at[1],
+            device_id=where,
+            device_id_type=pl.DeviceIdType.MESH,
+        )
+        copy.start()
+        started.append(copy)
+        return copy
+
+    barrier = pltpu.get_barrier_semaphore()
+    for step in range(1, bands):
+        pl.semaphore_signal(
+            barrier, inc=1, device_id=band_at(step)[1], device_id_type=pl.DeviceIdType.MESH
+        )
+    pl.semaphore_signal(barrier, inc=1, device_id=mate, device_id_type=pl.DeviceIdType.MESH)
+    pl.semaphore_wait(barrier, bands)
+
+    def swap_lon(source, leg):
+        return [
+            send(source.at[:, :, cs], other.at[leg, :, :, cs], lon_sem.at[leg, c], mate)
+            for c, cs in enumerate(chunks)
+        ]
+
+    def to_owner(source, leg, c, copy):
+        cs = chunks[c]
+        copy.wait_recv()
+
+        @pl.loop(0, rows)
+        def _(row):
+            summed = jnp.dot(
+                table_in[lon], source[row, :, cs], preferred_element_type=jnp.float32
+            ) + jnp.dot(
+                table_in[1 - lon], other[leg, row, :, cs], preferred_element_type=jnp.float32
+            )
+            at = pl.ds(pl.multiple_of(row * per_row, per_row), per_row)
+            sent[leg, :, at, cs] = (
+                (summed * scale).astype(jnp.bfloat16).reshape(bands, per_row, -1)
+            )
+
+        copies = []
+        for step in range(1, bands):
+            band, where = band_at(step)
+            copies.append(
+                send(
+                    sent.at[leg, band, :, cs],
+                    landed.at[leg, me, :, cs],
+                    go_sem.at[leg, c, step - 1],
+                    where,
+                )
+            )
+        landed[leg, me, :, cs] = sent[leg, me, :, cs]
+        return copies
+
+    def spectral(leg, c, copies):
+        cs = chunks[c]
+        tiles = cs.size // 128
+        for copy in copies:
+            copy.wait_recv()
+        for tile in range(tiles):
+            lanes = pl.ds(cs.start + tile * 128, 128)
+            strided_in[pl.ds(tile * total, total), :] = (
+                landed[leg, :, :, lanes].reshape(total, 128).astype(jnp.float32)
+            )
+
+        @pl.loop(0, modes)
+        def _(mode):
+            at = [pl.ds(tile * total + mode, 2 * rows * bands, stride=modes) for tile in range(tiles)]
+            source = jnp.concatenate([strided_in[a, :] for a in at], axis=1).astype(jnp.bfloat16)
+            eight = pl.ds(pl.multiple_of(mode * 8, 8), 8)
+            filt = pieces_f32[:, eight, :].reshape(bands * 8, pieces_f32.shape[2])
+            filt = filt[:, : 2 * rows * bands].astype(jnp.bfloat16)
+            if leg == 0:
+                source = jnp.dot(filt, source, preferred_element_type=jnp.float32)
+                source = source.astype(jnp.bfloat16)
+                first, second = left, right
+            else:
+                first, second = right_t, left_t
+            coeffs = jnp.dot(first[mode], source, preferred_element_type=jnp.float32)
+            degrees = coeffs.shape[0] // 2
+            gained = (coeffs.reshape(2, degrees, -1) * gain[:, cs][None]).astype(jnp.bfloat16)
+            result = jnp.dot(
+                second[mode],
+                gained.reshape(2 * degrees, -1),
+                preferred_element_type=jnp.float32,
+            )
+            if leg == 1:
+                result = lax.dot_general(
+                    filt,
+                    result.astype(jnp.bfloat16),
+                    (((0,), (0,)), ((), ())),
+                    preferred_element_type=jnp.float32,
+                )
+            for tile in range(tiles):
+                strided_out[at[tile], :] = result[:, tile * 128 : (tile + 1) * 128]
+
+        for tile in range(tiles):
+            lanes = pl.ds(cs.start + tile * 128, 128)
+            back_sent[leg, :, :, lanes] = (
+                strided_out[pl.ds(tile * total, total), :]
+                .astype(jnp.bfloat16)
+                .reshape(bands, width, 128)
+            )
+        back = []
+        for step in range(1, bands):
+            band, where = band_at(step)
+            back.append(
+                send(
+                    back_sent.at[leg, band, :, cs],
+                    back_landed.at[leg, me, :, cs],
+                    back_sem.at[leg, c, step - 1],
+                    where,
+                )
+            )
+        back_landed[leg, me, :, cs] = back_sent[leg, me, :, cs]
+        return back
+
+    def swap_back(leg, c, copies):
+        cs = chunks[c]
+        for copy in copies:
+            copy.wait_recv()
+        return send(
+            back_landed.at[leg, :, :, cs], back_other.at[leg, :, :, cs], swap_sem.at[leg, c], mate
+        )
+
+    def to_grid_rows(base, target, leg, c, copy):
+        cs = chunks[c]
+        copy.wait_recv()
+
+        @pl.loop(0, rows)
+        def _(row):
+            at = pl.ds(pl.multiple_of(row * per_row, per_row), per_row)
+            near = back_landed[leg, :, at, cs].reshape(bands * per_row, -1)
+            far = back_other[leg, :, at, cs].reshape(bands * per_row, -1)
+            summed = jnp.dot(
+                table_out[lon], near, preferred_element_type=jnp.float32
+            ) + jnp.dot(table_out[1 - lon], far, preferred_element_type=jnp.float32)
+            target[row, :, cs] = (base[row, :, cs].astype(jnp.float32) + summed * scale).astype(
+                jnp.bfloat16
+            )
+
+    count = range(len(chunks))
+    first_swap = swap_lon(field, 0)
+    piece_copies = []
+    for step in range(1, bands):
+        band, where = band_at(step)
+        piece_copies.append(
+            send(pieces.at[band], pieces_all.at[me], piece_sem.at[step - 1], where)
+        )
+    pieces_all[me] = pieces[me]
+    going = [to_owner(field, 0, c, first_swap[c]) for c in count]
+
+    held = win_own.shape[0]
+    mine = pl.ds(pl.multiple_of(chan * held, 16), held)
+    beside = {"chan": 1 - chan}
+    weight_copies = [
+        send(wout_own, wout.at[mine], weight_sem.at[0], beside),
+        send(win_own, win.at[mine], weight_sem.at[1], beside),
+    ]
+    win[mine, :] = win_own[...]
+    wout[mine, :] = wout_own[...]
+
+    for copy in piece_copies:
+        copy.wait_recv()
+    pieces_f32[...] = pieces_all[...].astype(jnp.float32)
+    coming = [spectral(0, c, going[c]) for c in count]
+    for copy in weight_copies:
+        copy.wait_recv()
+
+    @pl.loop(0, rows)
+    def _(row):
+        grad_act[row] = lax.dot_general(
+            cot[row], wout[...], (((1,), (1,)), ((), ())), preferred_element_type=jnp.float32
+        )
+
+    swapped = [swap_back(0, c, coming[c]) for c in count]
+    for c in count:
+        to_grid_rows(field, hidden, 0, c, swapped[c])
+
+    @pl.loop(0, rows)
+    def _(row):
+        pre_act = jnp.dot(hidden[row], win[...], preferred_element_type=jnp.float32)
+        grad_pre = (grad_act[row] * gelu_slope(pre_act)).astype(jnp.bfloat16)
+        back_rows = lax.dot_general(
+            grad_pre, win[...], (((1,), (1,)), ((), ())), preferred_element_type=jnp.float32
+        )
+        hidden[row] = (cot[row].astype(jnp.float32) + back_rows).astype(jnp.bfloat16)
+
+    second_swap = swap_lon(hidden, 1)
+    going = [to_owner(hidden, 1, c, second_swap[c]) for c in count]
+    coming = [spectral(1, c, going[c]) for c in count]
+    swapped = [swap_back(1, c, coming[c]) for c in count]
+    for c in count:
+        to_grid_rows(hidden, out, 1, c, swapped[c])
+    for copy in started:
+        copy.wait_send()
+
+
+def per_device(
+    field_in,
+    cotangent,
+    mlp_in_weight,
+    mlp_out_weight,
+    legendre_analysis,
+    legendre_synthesis,
+    spectral_gain,
+    disco_filter,
+    slot_pairs,
+    slot_count,
+):
+    chans = lax.axis_size("chan")
+    bands = lax.axis_size("lat") * chans
+    lon_local, rows, channels = field_in.shape
+    _, modes, degrees, all_rows = legendre_analysis.shape
+    lon = lax.axis_index("lon")
+    band = lax.axis_index(("lat", "chan"))
+    lon_pad = -(-lon_local // 16) * 16
+
+    def rows_first(grid_block):
+        return jnp.pad(
+            jnp.transpose(grid_block, (1, 0, 2)), ((0, 0), (0, lon_pad - lon_local), (0, 0))
+        )
+
+    cells = band_filter(disco_filter, slot_pairs, slot_count, rows)
+    span = 2 * REACH + 1
+    by_row = cells.reshape(rows, span, 2, bands, modes)
+    places = band * rows - REACH + jnp.arange(rows)[:, None] + jnp.arange(span)[None, :]
+    hits = (places[:, :, None] == jnp.arange(all_rows)).astype(jnp.bfloat16)
+    spread = jnp.einsum(
+        "rqpbm,rqi->pbmri", by_row, hits, preferred_element_type=jnp.float32
+    ).astype(jnp.bfloat16)
+    real, imag = spread[0], spread[1]
+    pieces = jnp.stack(
+        [jnp.stack([real, -imag], axis=-1), jnp.stack([imag, real], axis=-1)], axis=2
+    ).reshape(bands, modes, 2 * rows, 2 * all_rows)
+    lanes = -(-2 * all_rows // 128) * 128
+    pieces = jnp.pad(
+        pieces, ((0, 0), (0, 0), (0, 8 - 2 * rows), (0, lanes - 2 * all_rows))
+    ).reshape(bands, modes * 8, lanes)
+
+    both = jnp.eye(2, dtype=jnp.bfloat16)
+    analysis = legendre_analysis[0].reshape(modes, degrees, bands, rows)
+    synthesis = legendre_synthesis[0]
+    left = (analysis[:, None, :, :, None, :] * both[None, :, None, None, :, None]).reshape(
+        modes, 2, degrees, bands, 2 * rows
+    )
+    left = jnp.pad(left, ((0, 0),) * 4 + ((0, 8 - 2 * rows),)).reshape(
+        modes, 2 * degrees, bands * 8
+    )
+    right = (synthesis[:, :, None, None, :] * both[None, None, :, :, None]).reshape(
+        modes, 2 * all_rows, 2 * degrees
+    )
+    left_t = jnp.swapaxes(left, 1, 2)
+    right_t = jnp.swapaxes(right, 1, 2)
+    table = fixed_tables(bands, modes, lon_pad)
+    table_in = lax.dynamic_index_in_dim(jnp.asarray(table), lon, 0, keepdims=False)
+    table_out = lax.dynamic_index_in_dim(
+        jnp.asarray(table.transpose(1, 0, 3, 2)), lon, 0, keepdims=False
+    )
+
+    chunks = tuple(pl.ds(start, size) for start, size in split_channels(channels))
+    width = 2 * rows * modes
+    widest = max(chunk.size for chunk in chunks) // 128
+    held = (2, bands, width, channels)
+    grid_shape = (rows, lon_pad, channels)
+    bf16, f32 = jnp.bfloat16, jnp.float32
+    vmem = pl.BlockSpec(memory_space=pltpu.VMEM)
+    dma = pltpu.SemaphoreType.DMA
+    result = pl.pallas_call(
+        functools.partial(block_kernel, (bands, chans, rows, modes, channels, chunks)),
+        out_shape=jax.ShapeDtypeStruct(grid_shape, bf16),
+        in_specs=[vmem] * 12,
+        out_specs=vmem,
+        scratch_shapes=[
+            pltpu.VMEM((2,) + grid_shape, bf16),
+            pltpu.VMEM(held, bf16),
+            pltpu.VMEM(held, bf16),
+            pltpu.VMEM(held, bf16),
+            pltpu.VMEM(held, bf16),
+            pltpu.VMEM(held, bf16),
+            pltpu.VMEM(pieces.shape, bf16),
+            pltpu.VMEM(pieces.shape, f32),
+            pltpu.VMEM((widest * bands * width, 128), f32),
+            pltpu.VMEM((widest * bands * width, 128), f32),
+            pltpu.VMEM((channels, mlp_in_weight.shape[1]), bf16),
+            pltpu.VMEM((mlp_out_weight.shape[0] * chans, channels), bf16),
+            pltpu.VMEM((rows, lon_pad, mlp_in_weight.shape[1]), f32),
+            pltpu.VMEM(grid_shape, bf16),
+            dma((2, len(chunks), 2)),
+            dma((2, len(chunks), bands - 1, 2)),
+            dma((2, len(chunks), bands - 1, 2)),
+            dma((2, len(chunks), 2)),
+            dma((bands - 1, 2)),
+            dma((2, 2)),
+        ],
+        compiler_params=pltpu.CompilerParams(
+            collective_id=0, has_side_effects=True, vmem_limit_bytes=56 * 1024 * 1024
+        ),
+    )(
+        rows_first(field_in),
+        rows_first(cotangent),
+        mlp_in_weight,
+        mlp_out_weight,
+        pieces,
+        left,
+        right,
+        left_t,
+        right_t,
+        spectral_gain.astype(f32),
+        table_in,
+        table_out,
+    )
+    return jnp.transpose(result[:, :lon_local], (1, 0, 2))
+
+
+def split_channels(channels):
+    tiles = channels // 128
+    head = 128 * (tiles // 4 * 2 + tiles % 2)
+    return [(0, channels - head), (channels - head, head)] if 0 < head < channels else [(0, channels)]
+
+
 def solution(mesh):
+    owned = MODES // (mesh.shape["lon"] * mesh.shape["lat"] * mesh.shape["chan"])
+    fused = owned % 16 == 0 and mesh.shape["chan"] == 2 and mesh.shape["lon"] == 2
     return jax.shard_map(
-        per_device,
+        per_device if fused else per_device_plain,
         mesh=mesh,
         in_specs=(
             P(("groups", "lon"), ("lat", "chan"), None),

time: 250 us -> 143 us (0.57)
  blocking collectives: 128 us -> 0 us
  Pallas kernels: 0 us -> 120 us
  waiting for transfers between devices: 48.7 us -> 0 us
  matrix products: 31.5 us -> 0.42 us
  between operations: 14.3 us -> 0.89 us
  starting transfers between devices: 5.2 us -> 0 us
  local copies, waits for them, and re-layouts: 16.3 us -> 19 us
    pallas_call x0 -> x1, Pallas kernels: none -> 120 us  [per_device(): pl.pallas_call(functools.partial(block_kernel, (bands, chans, rows, modes...]
    all_to_all x3 -> x0, blocking collectives: 82.8 us -> none  [the longest x2 53.5 us: to_bands(): lax.all_to_all(owned_block, ('lat', 'chan'), split_axis=2, concat_axis=0,...]
    all_gather x3 -> x0, blocking collectives: 45.2 us -> none  [the longest x1 25.6 us: per_device(): all_cells = lax.all_gather(cells, ('lat', 'chan'), axis=0, tiled=True)]
    dot_general x10 -> x1, matrix products: 30.7 us -> 0.3 us  [per_device(): jnp.einsum('rqpbm,rqi->pbmri', by_row, hits, preferred_element_type=jnp.f...]
    all_gather x4 -> x0, waiting for transfers between devices: 28.3 us -> none  [the longest x2 16.9 us: to_spectrum(): piece_block = lax.all_gather(grid_block, 'lon', axis=0, tiled=True)]
    all_to_all x1 -> x0, waiting for transfers between devices: 19.7 us -> none  [to_owners(): lax.all_to_all(band_block, ('lat', 'chan'), split_axis=0, concat_axis=2,...]
    all_to_all x1 -> x0, starting transfers between devices: 5.07 us -> none  [to_owners(): lax.all_to_all(band_block, ('lat', 'chan'), split_axis=0, concat_axis=2,...]
    convert_element_type x8 -> x0, local copies, waits for them, and re-layouts: 4.82 us -> none  [the longest x4 3.04 us: to_spectrum(): return (summed * (1.0 / math.sqrt(NLON))).reshape((half_modes, 2) + tail_...]
  transfers between devices with their start and end apart: 5 -> 0, of which waited for: 3 -> 0; matrix products, arithmetic and copies ran while one was open for 4% -> 0% of each run, Pallas kernels for 0% -> 0%
where the time goes in v2:
time: 143 us
  Pallas kernels  120 us (84%)
  local copies, waits for them, and re-layouts  19 us (13%)
  other arithmetic  2.83 us (2%)
    pallas_call x1, Pallas kernels, per_device(): pl.pallas_call(functools.partial(block_kernel, (bands, chans, rows, modes...  120 us

profile of v2, /device:TPU:1, one launch (start us, length us, event | category | flops | bytes accessed | tf_op | source)
XLA Modules:
  0.0 143.0 jit_solution(11007655712507541743)
XLA Ops:
  0.7 0.8 add_bitcast_fusion
  1.6 0.1 copy.44
  1.8 0.1 convolution_convert_fusion.1
  2.2 0.3 fusion
  2.8 0.5 copy.39
  3.3 0.5 copy.51
  3.8 0.8 pad_bitcast_fusion.pieces
  4.7 0.1 copy.43
  4.8 0.8 broadcast_multiply_fusion.1
  5.7 1.0 pad.18
  6.8 0.8 reshape.91
  7.6 2.1 %dynamic-slice_bitcast_fusion.1.table_out = bf16[2,368,256]{2,1,0:T(8,128)(2,1)} fusion(bf16[2,2,368,256]{3,2,1,0:T(8,128)(2,1)} %constant.36.clone, s32[]{:T(128)S(6)} %select_n.6), kind=kLoop, calls=%fused_computation.8 | loop fusion | bytes 753668 | tf_op jit(solution)/shard_map/jit(dynamic_index_in_dim)/squeeze | solution.py:496
  9.7 0.8 dynamic-slice_bitcast_fusion.table_in
  10.5 0.9 convert_element_type.38.gain
  11.4 0.5 mul.72
  11.9 0.4 mul.73
  12.4 1.3 copy-done.3
  13.7 1.2 pad.15.field
  14.9 0.9 copy-done.4
  15.8 1.3 pad.16.cot
  17.1 1.7 %copy.45 = bf16[16,48,480]{1,2,0:T(8,128)(2,1)} copy(bf16[16,48,480]{2,1,0:T(8,128)(2,1)S(1)} %broadcast_multiply_fusion.right) | data formatting | bytes 1474560 | tf_op jit(solution)/shard_map/mul | solution.py:489
  18.8 1.8 %copy.46.left = bf16[16,480,64]{2,1,0:T(8,128)(2,1)} copy(bf16[16,480,64]{1,2,0:T(8,128)(2,1)S(1)} %reshape.91) | data formatting | bytes 1966080 | tf_op jit(solution)/shard_map/reshape | solution.py:486
  20.6 119.8 %shard_map.118 = bf16[3,368,640]{2,1,0:T(8,128)(2,1)} custom-call(bf16[3,368,640]{2,1,0:T(8,128)(2,1)} %pad.15.field, bf16[3,368,640]{2,1,0:T(8,128)(2,1)} %pad.16.cot, bf16[320,640]{1,0:T(8,128)(2,1)} %win_own.1, bf16[320,640]{1,0:T(8,128)(2,1)} %wout_own.1, bf16[8,128,128]{2,1,0:T(8,128)(2,1)} %pad_bitcast_fusion.pieces, bf16[16,480,64]{2,1,0:T(8,128)(2,1)} %copy.46.left, ...), custom_call_target="tpu_custom_call" | custom-call | tf_op jit(solution)/shard_map/pallas_call | solution.py:508
  140.5 2.5 %slice_bitcast_fusion = bf16[360,3,640]{2,0,1:T(8,128)(2,1)} fusion(bf16[3,368,640]{2,1,0:T(8,128)(2,1)} %shard_map.118), kind=kLoop, calls=%fused_computation | loop fusion | bytes 2764800 | tf_op jit(solution)/shard_map/transpose | solution.py:552
  (33 shorter events, 1.0 us)
Async XLA Ops:
  0.0 1.8 %copy-start = (bf16[15,2,128]{2,1,0:T(2,128)(2,1)S(1)}, bf16[15,2,128]{2,1,0:T(2,128)(2,1)}, u32[]{:S(2)}) copy-start(bf16[15,2,128]{2,1,0:T(2,128)(2,1)} %param.19) | copy-start | bytes 23044
  2.7 1.9 %copy-start.6 = (bf16[1,16,240,24]{2,3,1,0:T(8,128)(2,1)S(1)}, bf16[1,16,240,24]{2,3,1,0:T(8,128)(2,1)}, u32[]{:S(2)}) copy-start(bf16[1,16,240,24]{2,3,1,0:T(8,128)(2,1)} %param.16) | copy-start | bytes 552964
  6.7 3.0 %copy-start.7 = (bf16[2,2,256,368]{3,2,1,0:T(8,128)(2,1)S(1)}, bf16[2,2,256,368]{3,2,1,0:T(8,128)(2,1)}, u32[]{:S(2)}) copy-start(bf16[2,2,256,368]{3,2,1,0:T(8,128)(2,1)} %constant.35.clone) | copy-start | bytes 2260996
  6.7 3.8 %copy-start.5 = (bf16[240,640]{1,0:T(8,128)(2,1)S(1)}, bf16[240,640]{1,0:T(8,128)(2,1)}, u32[]{:S(2)}) copy-start(bf16[240,640]{1,0:T(8,128)(2,1)} %param.18) | copy-start | bytes 921604
  7.6 11.2 %copy-start.1 = (bf16[16,480,64]{1,2,0:T(8,128)(2,1)}, bf16[16,480,64]{1,2,0:T(8,128)(2,1)S(1)}, u32[]{:S(2)}) copy-start(bf16[16,480,64]{1,2,0:T(8,128)(2,1)S(1)} %reshape.91) | copy-start | bytes 2949124
  7.6 3.8 %copy-start.8 = (bf16[1,16,24,240]{3,2,1,0:T(8,128)(2,1)S(1)}, bf16[1,16,24,240]{3,2,1,0:T(8,128)(2,1)}, u32[]{:S(2)}) copy-start(bf16[1,16,24,240]{3,2,1,0:T(8,128)(2,1)} %param.17) | copy-start | bytes 552964
  12.3 1.3 copy-start.3
  13.7 3.4 %copy-start.2 = (bf16[16,48,480]{2,1,0:T(8,128)(2,1)}, bf16[16,48,480]{2,1,0:T(8,128)(2,1)S(1)}, u32[]{:S(2)}) copy-start(bf16[16,48,480]{2,1,0:T(8,128)(2,1)S(1)} %broadcast_multiply_fusion.right) | copy-start | bytes 2211844
  13.7 2.1 %copy-start.4 = (bf16[360,3,640]{2,0,1:T(8,128)(2,1)S(1)}, bf16[360,3,640]{2,0,1:T(8,128)(2,1)}, u32[]{:S(2)}) copy-start(bf16[360,3,640]{2,0,1:T(8,128)(2,1)} %param.13) | copy-start | bytes 4147204

commit v3 on v2

--- a/solution.py
+++ b/solution.py
@@ -190,15 +190,25 @@
     cot,
     win_own,
     wout_own,
-    pieces,
+    disco,
+    cell_places,
+    analysis,
+    synthesis,
+    to_eights,
+    to_pairs,
+    gain_in,
+    table_in,
+    table_out,
+    out,
+    field_pad,
+    gain,
     left,
     right,
     left_t,
     right_t,
-    gain,
-    table_in,
-    table_out,
-    out,
+    pieces,
+    pre_act,
+    grad_pre,
     other,
     sent,
     landed,
@@ -227,6 +237,7 @@
     lat, chan, lon = lax.axis_index("lat"), lax.axis_index("chan"), lax.axis_index("lon")
     me = lat * chans + chan
     mate = {"lon": 1 - lon}
+    lons = field.shape[1]
     scale = 1.0 / math.sqrt(NLON)
     started = []
 
@@ -255,11 +266,24 @@
     pl.semaphore_signal(barrier, inc=1, device_id=mate, device_id_type=pl.DeviceIdType.MESH)
     pl.semaphore_wait(barrier, bands)
 
-    def swap_lon(source, leg):
-        return [
-            send(source.at[:, :, cs], other.at[leg, :, :, cs], lon_sem.at[leg, c], mate)
-            for c, cs in enumerate(chunks)
-        ]
+    def swap_lon(source, leg, c):
+        cs = chunks[c]
+        return send(source.at[:, :, cs], other.at[leg, :, :, cs], lon_sem.at[leg, c], mate)
+
+    def stack_parts(wide, tall, wide_ref, tall_ref, wide_places, tall_places):
+        @pl.loop(0, modes, unroll=4)
+        def _(mode):
+            degrees = wide.shape[2]
+            for part in range(2):
+                wide_ref[mode, part] = jnp.dot(
+                    wide_places[part], wide[mode], preferred_element_type=jnp.float32
+                ).astype(jnp.bfloat16)
+                tall_ref[mode, part * degrees : (part + 1) * degrees, :] = lax.dot_general(
+                    tall[mode],
+                    tall_places[part],
+                    (((0,), (1,)), ((), ())),
+                    preferred_element_type=jnp.float32,
+                ).astype(jnp.bfloat16)
 
     def to_owner(source, leg, c, copy):
         cs = chunks[c]
@@ -268,9 +292,9 @@
         @pl.loop(0, rows)
         def _(row):
             summed = jnp.dot(
-                table_in[lon], source[row, :, cs], preferred_element_type=jnp.float32
+                table_in[lon, lon], source[row, :, cs], preferred_element_type=jnp.float32
             ) + jnp.dot(
-                table_in[1 - lon], other[leg, row, :, cs], preferred_element_type=jnp.float32
+                table_in[lon, 1 - lon], other[leg, row, :, cs], preferred_element_type=jnp.float32
             )
             at = pl.ds(pl.multiple_of(row * per_row, per_row), per_row)
             sent[leg, :, at, cs] = (
@@ -302,7 +326,7 @@
                 landed[leg, :, :, lanes].reshape(total, 128).astype(jnp.float32)
             )
 
-        @pl.loop(0, modes)
+        @pl.loop(0, modes, unroll=4)
         def _(mode):
             at = [pl.ds(tile * total + mode, 2 * rows * bands, stride=modes) for tile in range(tiles)]
             source = jnp.concatenate([strided_in[a, :] for a in at], axis=1).astype(jnp.bfloat16)
@@ -319,10 +343,8 @@
             degrees = coeffs.shape[0] // 2
             gained = (coeffs.reshape(2, degrees, -1) * gain[:, cs][None]).astype(jnp.bfloat16)
             result = jnp.dot(
-                second[mode],
-                gained.reshape(2 * degrees, -1),
-                preferred_element_type=jnp.float32,
-            )
+                second[mode, 0], gained[0], preferred_element_type=jnp.float32
+            ) + jnp.dot(second[mode, 1], gained[1], preferred_element_type=jnp.float32)
             if leg == 1:
                 result = lax.dot_general(
                     filt,
@@ -372,14 +394,33 @@
             near = back_landed[leg, :, at, cs].reshape(bands * per_row, -1)
             far = back_other[leg, :, at, cs].reshape(bands * per_row, -1)
             summed = jnp.dot(
-                table_out[lon], near, preferred_element_type=jnp.float32
-            ) + jnp.dot(table_out[1 - lon], far, preferred_element_type=jnp.float32)
-            target[row, :, cs] = (base[row, :, cs].astype(jnp.float32) + summed * scale).astype(
-                jnp.bfloat16
-            )
+                table_out[lon, lon], near, preferred_element_type=jnp.float32
+            ) + jnp.dot(table_out[lon, 1 - lon], far, preferred_element_type=jnp.float32)
+            moved = (base[row, :, cs].astype(jnp.float32) + summed * scale).astype(jnp.bfloat16)
+            target[row, :, cs] = moved[: target.shape[1]]
+            if leg == 0:
+                term = jnp.dot(moved[:lons], win[cs, :], preferred_element_type=jnp.float32)
+                pre_act[row] = term if c == 0 else pre_act[row] + term
 
     count = range(len(chunks))
-    first_swap = swap_lon(field, 0)
+    last = len(chunks) - 1
+    field_pad[:, field_pad.shape[1] - 16 :, :] = jnp.zeros(
+        (rows, 16, channels), field_pad.dtype
+    )
+    for row in range(rows):
+        field_pad[row, :lons, :] = field[row]
+    swaps = [swap_lon(field_pad, 0, c) for c in count]
+
+    for place in range(8):
+        strided_out[pl.ds(place, bands * modes, stride=8), :] = lax.dot_general(
+            disco[...],
+            cell_places[place],
+            (((0,), (0,)), ((), ())),
+            preferred_element_type=jnp.float32,
+        )
+    pieces[...] = (
+        strided_out[: bands * modes * 8, :].reshape(pieces.shape).astype(jnp.bfloat16)
+    )
     piece_copies = []
     for step in range(1, bands):
         band, where = band_at(step)
@@ -387,7 +428,7 @@
             send(pieces.at[band], pieces_all.at[me], piece_sem.at[step - 1], where)
         )
     pieces_all[me] = pieces[me]
-    going = [to_owner(field, 0, c, first_swap[c]) for c in count]
+    going = [to_owner(field_pad, 0, c, swaps[c]) for c in count]
 
     held = win_own.shape[0]
     mine = pl.ds(pl.multiple_of(chan * held, 16), held)
@@ -398,10 +439,12 @@
     ]
     win[mine, :] = win_own[...]
     wout[mine, :] = wout_own[...]
-
+    gain[...] = gain_in[...].astype(jnp.float32)
+    stack_parts(synthesis, analysis, right, left, to_pairs, to_eights)
     for copy in piece_copies:
         copy.wait_recv()
     pieces_f32[...] = pieces_all[...].astype(jnp.float32)
+
     coming = [spectral(0, c, going[c]) for c in count]
     for copy in weight_copies:
         copy.wait_recv()
@@ -412,25 +455,43 @@
             cot[row], wout[...], (((1,), (1,)), ((), ())), preferred_element_type=jnp.float32
         )
 
-    swapped = [swap_back(0, c, coming[c]) for c in count]
-    for c in count:
-        to_grid_rows(field, hidden, 0, c, swapped[c])
+    stack_parts(analysis, synthesis, left_t, right_t, to_eights, to_pairs)
+
+    def finish(leg, base, target):
+        swaps = [swap_back(leg, 0, coming[0])]
+        for c in count:
+            if c < last:
+                swaps.append(swap_back(leg, c + 1, coming[c + 1]))
+            to_grid_rows(base, target, leg, c, swaps[c])
+
+    finish(0, field_pad, hidden)
 
     @pl.loop(0, rows)
     def _(row):
-        pre_act = jnp.dot(hidden[row], win[...], preferred_element_type=jnp.float32)
-        grad_pre = (grad_act[row] * gelu_slope(pre_act)).astype(jnp.bfloat16)
-        back_rows = lax.dot_general(
-            grad_pre, win[...], (((1,), (1,)), ((), ())), preferred_element_type=jnp.float32
-        )
-        hidden[row] = (cot[row].astype(jnp.float32) + back_rows).astype(jnp.bfloat16)
-
-    second_swap = swap_lon(hidden, 1)
-    going = [to_owner(hidden, 1, c, second_swap[c]) for c in count]
+        grad_pre[row] = (grad_act[row] * gelu_slope(pre_act[row])).astype(jnp.bfloat16)
+
+    swaps, going = [], []
+    for c in count:
+        cs = chunks[c]
+
+        @pl.loop(0, rows)
+        def _(row):
+            back_rows = lax.dot_general(
+                grad_pre[row],
+                win[cs, :],
+                (((1,), (1,)), ((), ())),
+                preferred_element_type=jnp.float32,
+            )
+            hidden[row, :lons, cs] = (cot[row, :, cs].astype(jnp.float32) + back_rows).astype(
+                jnp.bfloat16
+            )
+
+        swaps.append(swap_lon(hidden, 1, c))
+        if c > 0:
+            going.append(to_owner(hidden, 1, c - 1, swaps[c - 1]))
+    going.append(to_owner(hidden, 1, last, swaps[last]))
     coming = [spectral(1, c, going[c]) for c in count]
-    swapped = [swap_back(1, c, coming[c]) for c in count]
-    for c in count:
-        to_grid_rows(hidden, out, 1, c, swapped[c])
+    finish(1, hidden, out)
     for copy in started:
         copy.wait_send()
 
@@ -451,79 +512,68 @@
     bands = lax.axis_size("lat") * chans
     lon_local, rows, channels = field_in.shape
     _, modes, degrees, all_rows = legendre_analysis.shape
-    lon = lax.axis_index("lon")
     band = lax.axis_index(("lat", "chan"))
     lon_pad = -(-lon_local // 16) * 16
 
-    def rows_first(grid_block):
-        return jnp.pad(
-            jnp.transpose(grid_block, (1, 0, 2)), ((0, 0), (0, lon_pad - lon_local), (0, 0))
-        )
-
-    cells = band_filter(disco_filter, slot_pairs, slot_count, rows)
-    span = 2 * REACH + 1
-    by_row = cells.reshape(rows, span, 2, bands, modes)
-    places = band * rows - REACH + jnp.arange(rows)[:, None] + jnp.arange(span)[None, :]
-    hits = (places[:, :, None] == jnp.arange(all_rows)).astype(jnp.bfloat16)
-    spread = jnp.einsum(
-        "rqpbm,rqi->pbmri", by_row, hits, preferred_element_type=jnp.float32
-    ).astype(jnp.bfloat16)
-    real, imag = spread[0], spread[1]
-    pieces = jnp.stack(
-        [jnp.stack([real, -imag], axis=-1), jnp.stack([imag, real], axis=-1)], axis=2
-    ).reshape(bands, modes, 2 * rows, 2 * all_rows)
+    slots = disco_filter.shape[0]
     lanes = -(-2 * all_rows // 128) * 128
-    pieces = jnp.pad(
-        pieces, ((0, 0), (0, 0), (0, 8 - 2 * rows), (0, lanes - 2 * all_rows))
-    ).reshape(bands, modes * 8, lanes)
-
-    both = jnp.eye(2, dtype=jnp.bfloat16)
-    analysis = legendre_analysis[0].reshape(modes, degrees, bands, rows)
-    synthesis = legendre_synthesis[0]
-    left = (analysis[:, None, :, :, None, :] * both[None, :, None, None, :, None]).reshape(
-        modes, 2, degrees, bands, 2 * rows
-    )
-    left = jnp.pad(left, ((0, 0),) * 4 + ((0, 8 - 2 * rows),)).reshape(
-        modes, 2 * degrees, bands * 8
-    )
-    right = (synthesis[:, :, None, None, :] * both[None, None, :, :, None]).reshape(
-        modes, 2 * all_rows, 2 * degrees
-    )
-    left_t = jnp.swapaxes(left, 1, 2)
-    right_t = jnp.swapaxes(right, 1, 2)
+    shape = (8, slots, 2, lanes)
+    place, slot, piece, lane = (lax.broadcasted_iota(jnp.int32, shape, d) for d in range(4))
+    slot_rows = slot_pairs[:, 0][None, :, None, None]
+    slot_from = slot_rows + slot_pairs[:, 1][None, :, None, None] + (band * rows - REACH)
+    part_out, part_in = place // rows, lane % 2
+    met = (slot < slot_count[0]) & (place % rows == slot_rows) & (lane // 2 == slot_from)
+    met = met & (place < 2 * rows) & (lane < 2 * all_rows) & ((part_out != part_in) == (piece == 1))
+    sign = jnp.where(part_out < part_in, -1.0, 1.0)
+    cell_places = jnp.where(met, sign, 0.0).astype(jnp.bfloat16).reshape(8, 2 * slots, lanes)
+
+    own_rows = np.arange(all_rows)
+    to_eights = np.zeros((2, bands * 8, all_rows), np.float32)
+    to_pairs = np.zeros((2, 2 * all_rows, all_rows), np.float32)
+    for part in range(2):
+        to_eights[part, own_rows // rows * 8 + part * rows + own_rows % rows, own_rows] = 1.0
+        to_pairs[part, 2 * own_rows + part, own_rows] = 1.0
     table = fixed_tables(bands, modes, lon_pad)
-    table_in = lax.dynamic_index_in_dim(jnp.asarray(table), lon, 0, keepdims=False)
-    table_out = lax.dynamic_index_in_dim(
-        jnp.asarray(table.transpose(1, 0, 3, 2)), lon, 0, keepdims=False
-    )
 
     chunks = tuple(pl.ds(start, size) for start, size in split_channels(channels))
     width = 2 * rows * modes
     widest = max(chunk.size for chunk in chunks) // 128
     held = (2, bands, width, channels)
     grid_shape = (rows, lon_pad, channels)
+    out_shape = (rows, lon_local, channels)
+    hidden_shape = (rows, lon_local, mlp_in_weight.shape[1])
+    pieces_shape = (bands, modes * 8, lanes)
     bf16, f32 = jnp.bfloat16, jnp.float32
     vmem = pl.BlockSpec(memory_space=pltpu.VMEM)
     dma = pltpu.SemaphoreType.DMA
     result = pl.pallas_call(
         functools.partial(block_kernel, (bands, chans, rows, modes, channels, chunks)),
-        out_shape=jax.ShapeDtypeStruct(grid_shape, bf16),
-        in_specs=[vmem] * 12,
+        out_shape=jax.ShapeDtypeStruct(out_shape, bf16),
+        in_specs=[vmem] * 13,
         out_specs=vmem,
         scratch_shapes=[
+            pltpu.VMEM(grid_shape, bf16),
+            pltpu.VMEM((degrees, channels), f32),
+            pltpu.VMEM((modes, 2 * degrees, bands * 8), bf16),
+            pltpu.VMEM((modes, 2, 2 * all_rows, degrees), bf16),
+            pltpu.VMEM((modes, 2, bands * 8, degrees), bf16),
+            pltpu.VMEM((modes, 2 * degrees, 2 * all_rows), bf16),
+            pltpu.VMEM(pieces_shape, bf16),
+            pltpu.VMEM(hidden_shape, f32),
+            pltpu.VMEM(hidden_shape, bf16),
             pltpu.VMEM((2,) + grid_shape, bf16),
             pltpu.VMEM(held, bf16),
             pltpu.VMEM(held, bf16),
             pltpu.VMEM(held, bf16),
             pltpu.VMEM(held, bf16),
             pltpu.VMEM(held, bf16),
-            pltpu.VMEM(pieces.shape, bf16),
-            pltpu.VMEM(pieces.shape, f32),
+            pltpu.VMEM(pieces_shape, bf16),
+            pltpu.VMEM(pieces_shape, f32),
             pltpu.VMEM((widest * bands * width, 128), f32),
             pltpu.VMEM((widest * bands * width, 128), f32),
             pltpu.VMEM((channels, mlp_in_weight.shape[1]), bf16),
             pltpu.VMEM((mlp_out_weight.shape[0] * chans, channels), bf16),
-            pltpu.VMEM((rows, lon_pad, mlp_in_weight.shape[1]), f32),
+            pltpu.VMEM(hidden_shape, f32),
             pltpu.VMEM(grid_shape, bf16),
             dma((2, len(chunks), 2)),
             dma((2, len(chunks), bands - 1, 2)),
@@ -536,26 +586,25 @@
             collective_id=0, has_side_effects=True, vmem_limit_bytes=56 * 1024 * 1024
         ),
     )(
-        rows_first(field_in),
-        rows_first(cotangent),
+        jnp.transpose(field_in, (1, 0, 2)),
+        jnp.transpose(cotangent, (1, 0, 2)),
         mlp_in_weight,
         mlp_out_weight,
-        pieces,
-        left,
-        right,
-        left_t,
-        right_t,
-        spectral_gain.astype(f32),
-        table_in,
-        table_out,
-    )
-    return jnp.transpose(result[:, :lon_local], (1, 0, 2))
+        disco_filter.reshape(2 * slots, bands * modes),
+        cell_places,
+        jnp.swapaxes(legendre_analysis[0], 1, 2),
+        legendre_synthesis[0],
+        jnp.asarray(to_eights, bf16),
+        jnp.asarray(to_pairs, bf16),
+        spectral_gain,
+        jnp.asarray(table),
+        jnp.asarray(table.transpose(1, 0, 3, 2)),
+    )
+    return jnp.transpose(result, (1, 0, 2))
 
 
 def split_channels(channels):
-    tiles = channels // 128
-    head = 128 * (tiles // 4 * 2 + tiles % 2)
-    return [(0, channels - head), (channels - head, head)] if 0 < head < channels else [(0, channels)]
+    return [(start, min(256, channels - start)) for start in range(0, channels, 256)]
 
 
 def solution(mesh):

time: 143 us -> 123 us (0.86)
  local copies, waits for them, and re-layouts: 19 us -> 5.12 us
  Pallas kernels: 120 us -> 115 us
    pallas_call x1, Pallas kernels: 120 us -> 115 us  [per_device(): pl.pallas_call(functools.partial(block_kernel, (bands, chans, rows, modes...]
    pad x3 -> x0, local copies, waits for them, and re-layouts: 3.54 us -> none  [the longest x2 2.49 us: rows_first(): jnp.pad(jnp.transpose(grid_block, (1, 0, 2)), ((0, 0), (0, lon_pad - lon_...]
    mul x11 -> x0, local copies, waits for them, and re-layouts: 3.3 us -> none  [the longest x5 2.83 us: per_device(): synthesis[:, :, None, None, :] * both[None, None, :, :, None]]
    squeeze x3 -> x0, local copies, waits for them, and re-layouts: 2.91 us -> none  [the longest x1 2.09 us: per_device(): lax.dynamic_index_in_dim(jnp.asarray(table.transpose(1, 0, 3, 2)), lon, 0...]
    transpose x1 -> x0, local copies, waits for them, and re-layouts: 2.54 us -> none  [per_device(): return jnp.transpose(result[:, :lon_local], (1, 0, 2))]
    reshape x4 -> x1, local copies, waits for them, and re-layouts: 3.48 us -> 1.31 us  [per_device(): disco_filter.reshape(2 * slots, bands * modes)]
where the time goes in v3:
time: 123 us
  Pallas kernels  115 us (93%)
  local copies, waits for them, and re-layouts  5.12 us (4%)
  other arithmetic  1.62 us (1%)
    pallas_call x1, Pallas kernels, per_device(): pl.pallas_call(functools.partial(block_kernel, (bands, chans, rows, modes...  115 us
    unnamed x1, local copies, waits for them, and re-layouts  2.54 us

profile of v3, /device:TPU:1, one launch (start us, length us, event | category | flops | bytes accessed | tf_op | source)
XLA Modules:
  0.0 122.9 jit_solution(11591101192446064155)
XLA Ops:
  0.7 0.8 fusion.6
  1.4 0.7 slice_bitcast_fusion
  2.2 0.1 iota.105
  2.3 0.1 iota.81
  2.4 0.1 iota.82
  2.5 0.1 eq.41
  2.6 0.1 eq.42
  2.6 0.1 eq.45
  2.7 0.1 eq.46
  2.8 1.3 %reshape.23.disco = bf16[30,128]{1,0:T(8,128)(2,1)} reshape(bf16[15,2,128]{2,1,0:T(2,128)(2,1)} %param.21) | data formatting | bytes 15360 | tf_op jit(solution)/shard_map/reshape | solution.py:593
  4.1 0.8 select_convert_fusion.cell_places
  4.9 115.4 %shard_map.136 = bf16[3,360,640]{2,1,0:T(8,128)(2,1)} custom-call(bf16[3,360,640]{2,1,0:T(8,128)(2,1)} %bitcast.18, bf16[3,360,640]{2,1,0:T(8,128)(2,1)} %bitcast.19, bf16[320,640]{1,0:T(8,128)(2,1)} %win_own.1, bf16[320,640]{1,0:T(8,128)(2,1)} %wout_own.1, bf16[30,128]{1,0:T(8,128)(2,1)} %reshape.23.disco, ...), custom_call_target="tpu_custom_call" | custom-call | tf_op jit(solution)/shard_map/pallas_call | solution.py:549
  120.4 2.5 %copy.17 = bf16[360,3,640]{2,0,1:T(8,128)(2,1)} copy(bf16[360,3,640]{2,0,1:T(8,128)(2,1)} %bitcast.17) | data formatting | bytes 2764800
  (11 shorter events, 0.1 us)

commit v4 on v3

--- a/solution.py
+++ b/solution.py
@@ -191,7 +191,8 @@
     win_own,
     wout_own,
     disco,
-    cell_places,
+    slot_pairs,
+    slot_count,
     analysis,
     synthesis,
     to_eights,
@@ -411,13 +412,29 @@
         field_pad[row, :lons, :] = field[row]
     swaps = [swap_lon(field_pad, 0, c) for c in count]
 
+    slots, all_rows = slot_pairs.shape[1], bands * rows
+    shape = (pieces.shape[2], slots)
+    lane = lax.broadcasted_iota(jnp.int32, shape, 0)
+    slot = lax.broadcasted_iota(jnp.int32, shape, 1)
+    slot_rows = jnp.broadcast_to(slot_pairs[0:1, :], shape)
+    slot_from = slot_rows + jnp.broadcast_to(slot_pairs[1:2, :], shape) + (me * rows - REACH)
+    part_in = lane % 2
+    met = (slot < slot_count[0]) & (lane // 2 == slot_from) & (lane < 2 * all_rows)
     for place in range(8):
-        strided_out[pl.ds(place, bands * modes, stride=8), :] = lax.dot_general(
-            disco[...],
-            cell_places[place],
-            (((0,), (0,)), ((), ())),
-            preferred_element_type=jnp.float32,
-        )
+        row_met = met & (slot_rows == place % rows) & (place < 2 * rows)
+        total_rows = 0.0
+        for piece in range(2):
+            part_out = place // rows
+            sign = jnp.where(part_in > part_out, -1.0, 1.0)
+            part_met = (part_in == part_out) if piece == 0 else (part_in != part_out)
+            cells = jnp.where(row_met & part_met, sign, 0.0).astype(jnp.bfloat16)
+            total_rows = total_rows + lax.dot_general(
+                disco[:, piece, :],
+                cells,
+                (((0,), (1,)), ((), ())),
+                preferred_element_type=jnp.float32,
+            )
+        strided_out[pl.ds(place, bands * modes, stride=8), :] = total_rows
     pieces[...] = (
         strided_out[: bands * modes * 8, :].reshape(pieces.shape).astype(jnp.bfloat16)
     )
@@ -512,21 +529,9 @@
     bands = lax.axis_size("lat") * chans
     lon_local, rows, channels = field_in.shape
     _, modes, degrees, all_rows = legendre_analysis.shape
-    band = lax.axis_index(("lat", "chan"))
     lon_pad = -(-lon_local // 16) * 16
 
-    slots = disco_filter.shape[0]
     lanes = -(-2 * all_rows // 128) * 128
-    shape = (8, slots, 2, lanes)
-    place, slot, piece, lane = (lax.broadcasted_iota(jnp.int32, shape, d) for d in range(4))
-    slot_rows = slot_pairs[:, 0][None, :, None, None]
-    slot_from = slot_rows + slot_pairs[:, 1][None, :, None, None] + (band * rows - REACH)
-    part_out, part_in = place // rows, lane % 2
-    met = (slot < slot_count[0]) & (place % rows == slot_rows) & (lane // 2 == slot_from)
-    met = met & (place < 2 * rows) & (lane < 2 * all_rows) & ((part_out != part_in) == (piece == 1))
-    sign = jnp.where(part_out < part_in, -1.0, 1.0)
-    cell_places = jnp.where(met, sign, 0.0).astype(jnp.bfloat16).reshape(8, 2 * slots, lanes)
-
     own_rows = np.arange(all_rows)
     to_eights = np.zeros((2, bands * 8, all_rows), np.float32)
     to_pairs = np.zeros((2, 2 * all_rows, all_rows), np.float32)
@@ -549,7 +554,7 @@
     result = pl.pallas_call(
         functools.partial(block_kernel, (bands, chans, rows, modes, channels, chunks)),
         out_shape=jax.ShapeDtypeStruct(out_shape, bf16),
-        in_specs=[vmem] * 13,
+        in_specs=[vmem] * 6 + [pl.BlockSpec(memory_space=pltpu.SMEM)] + [vmem] * 7,
         out_specs=vmem,
         scratch_shapes=[
             pltpu.VMEM(grid_shape, bf16),
@@ -590,8 +595,9 @@
         jnp.transpose(cotangent, (1, 0, 2)),
         mlp_in_weight,
         mlp_out_weight,
-        disco_filter.reshape(2 * slots, bands * modes),
-        cell_places,
+        disco_filter,
+        jnp.transpose(slot_pairs),
+        slot_count,
         jnp.swapaxes(legendre_analysis[0], 1, 2),
         legendre_synthesis[0],
         jnp.asarray(to_eights, bf16),

time: 123 us -> 119 us (0.967)
  local copies, waits for them, and re-layouts: 5.12 us -> 2.54 us
  other arithmetic: 1.62 us -> 0 us
    reshape x1 -> x0, local copies, waits for them, and re-layouts: 1.31 us -> none  [per_device(): disco_filter.reshape(2 * slots, bands * modes)]
where the time goes in v4:
time: 119 us
  Pallas kernels  115 us (97%)
  local copies, waits for them, and re-layouts  2.54 us (2%)
    pallas_call x1, Pallas kernels, per_device(): pl.pallas_call(functools.partial(block_kernel, (bands, chans, rows, modes...  115 us
    unnamed x1, local copies, waits for them, and re-layouts  2.54 us

profile of v4, /device:TPU:1, one launch (start us, length us, event | category | flops | bytes accessed | tf_op | source)
XLA Modules:
  0.0 118.7 jit_solution(8727758679334750981)
XLA Ops:
  0.7 115.5 %shard_map.136 = bf16[3,360,640]{2,1,0:T(8,128)(2,1)} custom-call(bf16[3,360,640]{2,1,0:T(8,128)(2,1)} %bitcast.9, bf16[3,360,640]{2,1,0:T(8,128)(2,1)} %bitcast.10, bf16[320,640]{1,0:T(8,128)(2,1)} %win_own.1, bf16[320,640]{1,0:T(8,128)(2,1)} %wout_own.1, bf16[15,2,128]{2,1,0:T(2,128)(2,1)} %disco.1, s32[2,15]{1,0:T(2,128)} %bitcast.13, ...), custom_call_target="tpu_custom_call" | custom-call | tf_op jit(solution)/shard_map/pallas_call | solution.py:554
  116.1 2.5 %copy.17 = bf16[360,3,640]{2,0,1:T(8,128)(2,1)} copy(bf16[360,3,640]{2,0,1:T(8,128)(2,1)} %bitcast.8) | data formatting | bytes 2764800
